TPU v7x, 32 devices: a whole 2x2x4 slice. The times are simulated.
32 devices in a mesh: replica: 8 (over y, x, core), shard: 4 (over z).
Axes of the slice: x: 2, y: 2, z: 4, core: 2. Of those that a mesh axis runs over, the one named last changes fastest.
Arguments:
- tokens: bfloat16 [32768, 768], P(('replica', 'shard')), may hold values from -6 to 6
- cotangent: bfloat16 [32768, 768], P(('replica', 'shard')), may hold values from -6 to 6
- segments: int32 [32, 1024], P(('replica', 'shard')), may hold values from 0 to 3, never falling along the last dimension, each value on 1 to 512 neighbouring positions
- routes: int32 [32768, 1], P(('replica', 'shard')), may hold values from 0 to 3; in each aligned block of 1024 rows (0 to 1023, 1024 to 2047, ...) at most 320 rows name the same one
- w_query: bfloat16 [768, 768], P('shard'), may hold values from -0.02734375 to 0.02734375
- w_key: bfloat16 [768, 768], P('shard'), may hold values from -0.21875 to 0.21875
- w_value: bfloat16 [768, 768], P('shard'), may hold values from -0.21875 to 0.21875
- w_output: bfloat16 [768, 768], P('shard'), may hold values from -1.75 to 1.75
- norm_attn: bfloat16 [768], P('shard'), may hold values from 0.5 to 1.5
- norm_ffn: bfloat16 [768], P('shard'), may hold values from 0.5 to 1.5
- w_router: bfloat16 [768, 4], P('shard'), may hold values from -0.15625 to 0.15625
- rel_bias: bfloat16 [32, 12], P('shard'), may hold values from -4 to 4
- expert_input_weight: bfloat16 [4, 768, 3072], P('shard'), may hold values from -0.21875 to 0.21875
- expert_output_weight: bfloat16 [4, 3072, 768], P('shard'), may hold values from -0.4375 to 0.4375
Outputs:
- mixed: bfloat16 [32768, 768], P(('replica', 'shard'))
- grad_tokens: float32 [32768, 768], P(('replica', 'shard'))
- grad_query: float32 [768, 768], P('shard')
- grad_key: float32 [768, 768], P('shard')
- grad_value: float32 [768, 768], P('shard')
- grad_output: float32 [768, 768], P('shard')
- grad_norm_attn: float32 [768], P('shard')
- grad_norm_ffn: float32 [768], P('shard')
- grad_router: float32 [768, 4], P('shard')
- grad_rel_bias: float32 [32, 12], P('shard')
- grad_expert_in: float32 [4, 768, 3072], P('shard')
- grad_expert_out: float32 [4, 3072, 768], P('shard')
Inputs may be any that keep to these rules, and one draw needn't show every extreme that they name: `segments`: within a sequence the segment numbers never fall; each of the 4 numbers covers 1 to 512 positions, and one covers exactly 512. `routes`: among the 1024 rows of one device no expert is named more than 320 times, and in some device's rows an expert is named exactly 320 times; every expert is named somewhere.
All inputs are finite; a program needn't handle non-finite values.
Results may differ from a plain program's by a relative error of at most 0.014.
Values may be sent and summed in bfloat16 or wider, within the bound.
No kernel may reach another device: no remote copies, remote signals or barrier semaphores. Data moves between devices by JAX's collectives and lax.ppermute only.
A program may use at most 320 MiB of HBM per device.

v0:
```python
from functools import partial

import jax
import jax.numpy as jnp
from jax import lax
from jax.sharding import PartitionSpec as P

highest = lax.Precision.HIGHEST
far_steps = (12, 16, 23, 32, 46, 64, 91)


def bucket_table(query_pos, key_pos):
    relative = key_pos[None, :] - query_pos[:, None]
    distance = jnp.abs(relative)
    beyond = jnp.zeros_like(distance)
    for threshold in far_steps:
        beyond = beyond + (distance >= threshold).astype(jnp.int32)
    inside = jnp.where(distance < 8, distance, 8 + beyond)
    return inside + 16 * (relative > 0).astype(jnp.int32)


def rms_norm(values_in, gain_vec):
    return (
        values_in
        * lax.rsqrt(jnp.mean(values_in * values_in, axis=-1, keepdims=True) + 1e-06)
        * gain_vec
    )


def block_scores(queries, key_rows, relative_bias_table, slot_indicators, allowed):
    raw_dot = jnp.einsum("qhe,khe->hqk", queries, key_rows, preferred_element_type=jnp.float32)
    relative_bias_term = jnp.einsum(
        "rni,rf->fni", slot_indicators, relative_bias_table, preferred_element_type=jnp.float32
    )
    scores = raw_dot + relative_bias_term
    return jnp.where(allowed[None], scores, -1e30)


def expert_forward(rows_in, first_all, second_all):
    before_activation = jnp.einsum(
        "ecd,edf->ecf", rows_in, first_all, preferred_element_type=jnp.float32
    )
    hidden = jax.nn.gelu(before_activation).astype(jnp.bfloat16)
    result = jnp.einsum(
        "ecf,efd->ecd", hidden, second_all, preferred_element_type=jnp.float32
    ).astype(jnp.bfloat16)
    return (before_activation, hidden, result)


def expert_backward(rows_in, before_activation, hidden, grad_result, first_all, second_all):
    grad_hidden = jnp.einsum(
        "ecd,efd->ecf", grad_result, second_all, preferred_element_type=jnp.float32
    )
    grad_second = jnp.einsum(
        "ecf,ecd->efd", hidden, grad_result, preferred_element_type=jnp.float32
    )
    grad_pre = jax.vjp(jax.nn.gelu, before_activation)[1](grad_hidden)[0].astype(jnp.bfloat16)
    grad_first = jnp.einsum("ecd,ecf->edf", rows_in, grad_pre, preferred_element_type=jnp.float32)
    grad_rows = jnp.einsum(
        "ecf,edf->ecd", grad_pre, first_all, preferred_element_type=jnp.float32
    ).astype(jnp.bfloat16)
    return (grad_first, grad_second, grad_rows)


def on_device(
    tokens,
    cotangent,
    segments,
    routes,
    w_query,
    w_key,
    w_value,
    w_output,
    norm_attn,
    norm_ffn,
    w_router,
    rel_bias,
    expert_input_weight,
    expert_output_weight,
):
    gathered = (
        lax.all_gather(w_query, "shard", axis=0, tiled=True),
        lax.all_gather(w_key, "shard", axis=0, tiled=True),
        lax.all_gather(w_value, "shard", axis=0, tiled=True),
        lax.all_gather(w_output, "shard", axis=0, tiled=True),
        lax.all_gather(norm_attn, "shard", axis=0, tiled=True),
        lax.all_gather(norm_ffn, "shard", axis=0, tiled=True),
        lax.all_gather(w_router, "shard", axis=0, tiled=True),
        lax.all_gather(rel_bias, "shard", axis=0, tiled=True),
    )
    (
        full_query,
        full_key,
        full_value,
        full_output,
        gain_one,
        gain_two,
        router,
        relative_bias_table,
    ) = gathered
    seq_count, length = segments.shape
    row_count, model_width = tokens.shape
    bucket_count, head_count = relative_bias_table.shape
    head_width = model_width // head_count
    experts = router.shape[1]
    qblock = min(512, length)
    positions = jnp.arange(length, dtype=jnp.int32)
    labels = jnp.arange(bucket_count, dtype=jnp.int32)

    def block_frame(which, offset):
        query_pos = positions[offset : offset + qblock]
        matches = bucket_table(query_pos, positions)[None] == labels[:, None, None]
        segment_row = segments[which]
        allowed = segment_row[offset : offset + qblock][:, None] == segment_row[None, :]
        return (matches, allowed)

    inputs = tokens.astype(jnp.float32)
    gain_one_f = gain_one.astype(jnp.float32)
    normed_one = rms_norm(inputs, gain_one_f).astype(jnp.bfloat16)

    def project(weight_mat):
        product = jnp.dot(normed_one, weight_mat, preferred_element_type=jnp.float32)
        return product.astype(jnp.bfloat16).reshape(seq_count, length, head_count, head_width)

    queries = project(full_query)
    key_rows = project(full_key)
    value_rows = project(full_value)
    pieces = []
    log_sums = []
    which = 0
    for offset in range(0, length, qblock):
        matches, allowed = block_frame(which, offset)
        scores = block_scores(
            queries[which, offset : offset + qblock],
            key_rows[which],
            relative_bias_table,
            matches.astype(jnp.bfloat16),
            allowed,
        )
        highest_score = jnp.max(scores, axis=-1, keepdims=True)
        shifted = jnp.exp(scores - highest_score)
        denominator = jnp.sum(shifted, axis=-1, keepdims=True)
        chances = (shifted / denominator).astype(jnp.bfloat16)
        log_sums.append(highest_score + jnp.log(denominator))
        pieces.append(
            jnp.einsum(
                "hqk,khe->qhe", chances, value_rows[which], preferred_element_type=jnp.float32
            )
        )
    attended = jnp.concatenate(pieces, 0).reshape(row_count, model_width).astype(jnp.bfloat16)
    branch = jnp.dot(attended, full_output, preferred_element_type=jnp.float32)
    middle = inputs + branch
    gain_two_f = gain_two.astype(jnp.float32)
    normed_two = rms_norm(middle, gain_two_f).astype(jnp.bfloat16)
    normed_two_f = normed_two.astype(jnp.float32)
    router_f = router.astype(jnp.float32)
    logits = jnp.dot(normed_two_f, router_f, precision=highest)
    gate_probs = jax.nn.softmax(logits, axis=-1)
    chosen = (routes == jnp.arange(experts, dtype=jnp.int32)[None, :]).astype(jnp.int32)
    chosen_f = chosen.astype(jnp.float32)
    chosen_gate = jnp.sum(gate_probs * chosen_f, axis=-1)
    slot_index = jnp.cumsum(chosen, axis=0) - chosen
    capacity = 5 * row_count // (4 * experts)
    slot_range = jnp.arange(capacity, dtype=jnp.int32)
    places = (
        (chosen.T[:, None, :] == 1) & (slot_index.T[:, None, :] == slot_range[None, :, None])
    ).astype(jnp.bfloat16)
    outgoing = jnp.einsum(
        "ect,td->ecd", places, normed_two, preferred_element_type=jnp.float32
    ).astype(jnp.bfloat16)
    arrived = lax.all_to_all(outgoing, "shard", split_axis=0, concat_axis=1, tiled=True)
    before_activation, hidden, result = expert_forward(
        arrived, expert_input_weight, expert_output_weight
    )
    returned = lax.all_to_all(result, "shard", split_axis=1, concat_axis=0, tiled=True)
    combined = jnp.einsum("ect,ecd->td", places, returned, preferred_element_type=jnp.float32)
    mixed_out = (middle + chosen_gate[:, None] * combined).astype(jnp.bfloat16)
    again = (
        lax.all_gather(w_query, "shard", axis=0, tiled=True),
        lax.all_gather(w_key, "shard", axis=0, tiled=True),
        lax.all_gather(w_value, "shard", axis=0, tiled=True),
        lax.all_gather(w_output, "shard", axis=0, tiled=True),
        lax.all_gather(norm_attn, "shard", axis=0, tiled=True),
        lax.all_gather(norm_ffn, "shard", axis=0, tiled=True),
        lax.all_gather(w_router, "shard", axis=0, tiled=True),
        lax.all_gather(rel_bias, "shard", axis=0, tiled=True),
    )
    (
        full_query,
        full_key,
        full_value,
        full_output,
        gain_one,
        gain_two,
        router,
        relative_bias_table,
    ) = again
    gain_one_f = gain_one.astype(jnp.float32)
    gain_two_f = gain_two.astype(jnp.float32)
    router_f = router.astype(jnp.float32)
    grad_final = cotangent.astype(jnp.float32)
    grad_gate = jnp.sum(grad_final * combined, axis=-1)
    scaled = (chosen_gate[:, None] * grad_final).astype(jnp.bfloat16)
    grad_slots = jnp.einsum(
        "ect,td->ecd", places, scaled, preferred_element_type=jnp.float32
    ).astype(jnp.bfloat16)
    grad_arrived = lax.all_to_all(grad_slots, "shard", split_axis=0, concat_axis=1, tiled=True)
    grad_first, grad_second, grad_rows = expert_backward(
        arrived, before_activation, hidden, grad_arrived, expert_input_weight, expert_output_weight
    )
    grad_back = lax.all_to_all(grad_rows, "shard", split_axis=1, concat_axis=0, tiled=True)
    grad_normed_two = jnp.einsum(
        "ect,ecd->td", places, grad_back, preferred_element_type=jnp.float32
    )
    grad_probs_gate = chosen_f * grad_gate[:, None]
    grad_logits = jax.vjp(partial(jax.nn.softmax, axis=-1), logits)[1](grad_probs_gate)[0]
    grad_router = jnp.dot(normed_two_f.T, grad_logits, precision=highest)
    grad_normed_two = grad_normed_two + jnp.dot(grad_logits, router_f.T, precision=highest)
    pull_two = jax.vjp(rms_norm, middle, gain_two_f)[1]
    grad_mid_norm, grad_gain_two = pull_two(grad_normed_two)
    grad_middle = grad_final + grad_mid_norm
    gradient_residual_branch = grad_middle.astype(jnp.bfloat16)
    grad_wout = jnp.einsum(
        "td,te->de", attended, gradient_residual_branch, preferred_element_type=jnp.float32
    )
    grad_attended = jnp.einsum(
        "te,de->td", gradient_residual_branch, full_output, preferred_element_type=jnp.float32
    )
    grad_attended = grad_attended.astype(jnp.bfloat16).reshape(
        seq_count, length, head_count, head_width
    )
    query_grads = []
    grad_table = jnp.zeros((bucket_count, head_count), jnp.float32)
    block_index = 0
    which = 0
    key_acc = jnp.zeros((length, head_count, head_width), jnp.float32)
    value_acc = jnp.zeros((length, head_count, head_width), jnp.float32)
    for offset in range(0, length, qblock):
        matches, allowed = block_frame(which, offset)
        query_part = queries[which, offset : offset + qblock]
        scores = block_scores(
            query_part, key_rows[which], relative_bias_table, matches.astype(jnp.bfloat16), allowed
        )
        chances = jnp.exp(scores - log_sums[block_index])
        grad_part = grad_attended[which, offset : offset + qblock]
        value_acc = value_acc + jnp.einsum(
            "hqk,qhe->khe",
            chances.astype(jnp.bfloat16),
            grad_part,
            preferred_element_type=jnp.float32,
        )
        grad_chances = jnp.einsum(
            "qhe,khe->hqk", grad_part, value_rows[which], preferred_element_type=jnp.float32
        )
        inner_sum = jnp.sum(chances * grad_chances, axis=-1, keepdims=True)
        grad_scores = chances * (grad_chances - inner_sum)
        grad_table = grad_table + jnp.einsum(
            "vsi,dsi->dv",
            grad_scores,
            matches.astype(jnp.float32),
            precision=highest,
            preferred_element_type=jnp.float32,
        )
        grad_raw = grad_scores.astype(jnp.bfloat16)
        query_grads.append(
            jnp.einsum(
                "hqk,khe->qhe", grad_raw, key_rows[which], preferred_element_type=jnp.float32
            )
        )
        key_acc = key_acc + jnp.einsum(
            "hqk,qhe->khe", grad_raw, query_part, preferred_element_type=jnp.float32
        )
        block_index = block_index + 1
    key_grads = [key_acc]
    value_grads = [value_acc]
    grad_q = jnp.concatenate(query_grads, 0).reshape(row_count, model_width).astype(jnp.bfloat16)
    grad_k = jnp.stack(key_grads).reshape(row_count, model_width).astype(jnp.bfloat16)
    grad_v = jnp.stack(value_grads).reshape(row_count, model_width).astype(jnp.bfloat16)
    grad_wq = jnp.einsum("td,te->de", normed_one, grad_q, preferred_element_type=jnp.float32)
    grad_wk = jnp.einsum("td,te->de", normed_one, grad_k, preferred_element_type=jnp.float32)
    grad_wv = jnp.einsum("td,te->de", normed_one, grad_v, preferred_element_type=jnp.float32)
    grad_normed_one = jnp.einsum(
        "te,de->td", grad_q, full_query, preferred_element_type=jnp.float32
    )
    grad_normed_one = grad_normed_one + jnp.einsum(
        "te,de->td", grad_k, full_key, preferred_element_type=jnp.float32
    )
    grad_normed_one = grad_normed_one + jnp.einsum(
        "te,de->td", grad_v, full_value, preferred_element_type=jnp.float32
    )
    pull_one = jax.vjp(rms_norm, inputs, gain_one_f)[1]
    grad_in_norm, grad_gain_one = pull_one(grad_normed_one)
    grad_inputs = grad_middle + grad_in_norm
    owned_grads = (
        lax.psum_scatter(grad_wq, "shard", scatter_dimension=0, tiled=True),
        lax.psum_scatter(grad_wk, "shard", scatter_dimension=0, tiled=True),
        lax.psum_scatter(grad_wv, "shard", scatter_dimension=0, tiled=True),
        lax.psum_scatter(grad_wout, "shard", scatter_dimension=0, tiled=True),
        lax.psum_scatter(grad_gain_one, "shard", scatter_dimension=0, tiled=True),
        lax.psum_scatter(grad_gain_two, "shard", scatter_dimension=0, tiled=True),
        lax.psum_scatter(grad_router, "shard", scatter_dimension=0, tiled=True),
        lax.psum_scatter(grad_table, "shard", scatter_dimension=0, tiled=True),
    )
    summed_grads = lax.psum(
        (
            owned_grads[0],
            owned_grads[1],
            owned_grads[2],
            owned_grads[3],
            owned_grads[4],
            owned_grads[5],
            owned_grads[6],
            owned_grads[7],
        ),
        "replica",
    )
    replica_parts = (
        lax.psum_scatter(grad_first, "replica", scatter_dimension=2, tiled=True),
        lax.psum_scatter(grad_second, "replica", scatter_dimension=1, tiled=True),
    )
    total_first, total_second = (
        lax.all_gather(replica_parts[0], "replica", axis=2, tiled=True),
        lax.all_gather(replica_parts[1], "replica", axis=1, tiled=True),
    )
    return (
        mixed_out,
        grad_inputs,
        summed_grads[0],
        summed_grads[1],
        summed_grads[2],
        summed_grads[3],
        summed_grads[4],
        summed_grads[5],
        summed_grads[6],
        summed_grads[7],
        total_first,
        total_second,
    )


def solution(mesh):
    placed = (
        P(("replica", "shard"), None),
        P(("replica", "shard"), None),
        P(("replica", "shard"), None),
        P(("replica", "shard"), None),
        P("shard", None),
        P("shard", None),
        P("shard", None),
        P("shard", None),
        P("shard"),
        P("shard"),
        P("shard", None),
        P("shard", None),
        P("shard", None, None),
        P("shard", None, None),
    )
    return jax.shard_map(
        on_device,
        mesh=mesh,
        in_specs=placed,
        out_specs=(
            P(("replica", "shard"), None),
            P(("replica", "shard"), None),
            P("shard", None),
            P("shard", None),
            P("shard", None),
            P("shard", None),
            P("shard"),
            P("shard"),
            P("shard", None),
            P("shard", None),
            P("shard", None, None),
            P("shard", None, None),
        ),
        check_vma=False,
    )
```

profile of v0, /device:TPU:0, one launch (start us, length us, event | category | flops | bytes accessed | tf_op | source)
XLA Modules:
  0.0 1068.2 jit_solution(8149581946401056184)
XLA Ops:
  13.6 13.6 %all-reduce.8 = (bf16[768]{0:T(1024)(128)(2,1)S(1)}, bf16[768]{0:T(1024)(128)(2,1)S(1)}) all-reduce(bf16[768]{0:T(1024)(128)(2,1)S(1)} %dynamic-update-slice, bf16[768]{0:T(1024)(128)(2,1)S(1)} %dynamic-update-slice.1), channel_id=1, replica_groups=mesh['replica'=8,'shard'=4] {'shard'}, use_global_device_ids=true, to_apply=%add | all-reduce | flops 1536 | bytes 6144
  29.9 12.1 %all_gather.42 = bf16[32,12]{1,0:T(8,128)(2,1)S(1)} all-gather(bf16[8,12]{1,0:T(8,128)(2,1)} %param.25), channel_id=1, replica_groups=mesh['replica'=8,'shard'=4] {'shard'}, dimensions={0}, use_global_device_ids=true | all-gather | bytes 960 | tf_op jit(solution)/shard_map/all_gather | solution.py:89
  54.6 16.3 %fusion.1 = f32[512,1024,12]{0,2,1:T(8,128)} fusion(s32[512,1024]{0,1:T(8,128)S(1)} %fusion.85, bf16[32,12]{1,0:T(8,128)(2,1)S(1)} %all_gather.42), kind=kOutput, calls=%fused_computation.2 | convolution fusion | flops 419430400 | bytes 27263744 | tf_op jit(solution)/shard_map/rni,rf->fni/dot_general | solution.py:32
  70.9 29.9 %copy.81 = f32[512,1024,12]{1,0,2:T(8,128)} copy(f32[512,1024,12]{0,2,1:T(8,128)} %fusion.1) | data formatting | bytes 50331648 | tf_op jit(solution)/shard_map/rni,rf->fni/dot_general | solution.py:32
  100.9 16.5 %fusion.3 = f32[512,1024,12]{0,2,1:T(8,128)} fusion(s32[512,1024]{0,1:T(8,128)S(1)} %fusion.84, bf16[32,12]{1,0:T(8,128)(2,1)S(1)} %all_gather.42), kind=kOutput, calls=%fused_computation.5 | convolution fusion | flops 419430400 | bytes 27263744 | tf_op jit(solution)/shard_map/rni,rf->fni/dot_general | solution.py:32
  117.4 30.6 %copy.80 = f32[512,1024,12]{1,0,2:T(8,128)} copy(f32[512,1024,12]{0,2,1:T(8,128)} %fusion.3) | data formatting | bytes 50331648 | tf_op jit(solution)/shard_map/rni,rf->fni/dot_general | solution.py:32
  156.3 16.6 %fusion.161 = (f32[12,512]{1,0:T(8,128)S(1)}, f32[12,512,1024]{2,1,0:T(8,128)}) fusion(f32[512,1024,12]{1,0,2:T(8,128)} %copy.81, bf16[1024,12,64]{0,2,1:T(8,128)(2,1)S(1)} %bitcast.170, bf16[1,1024,12,64]{1,3,2,0:T(8,128)(2,1)} %bitcast.190, pred[512,1024]{1,0:T(8,128)(4,1)} %get-tuple-element.82), kind=kOutput, calls=%fused_computation.199 | convolution fusion | flops 824174592 | bytes 53239808 | tf_op jit(solution)/shard_map/qhe,khe->hqk/dot_general | solution.py:31
  172.9 11.4 %fusion.11 = f32[12,512]{1,0:T(8,128)S(1)} fusion(f32[12,512,1024]{2,1,0:T(8,128)} %get-tuple-element.88, f32[12,512]{1,0:T(8,128)S(1)} %get-tuple-element.87), kind=kLoop, calls=%fused_computation.27 | loop fusion | flops 12576768 | bytes 25214976 | tf_op jit(solution)/shard_map/reduce_sum | solution.py:142
  187.2 12.0 %fusion.133 = bf16[512,12,64]{0,2,1:T(8,128)(2,1)} fusion(bf16[1024,12,64]{0,2,1:T(8,128)(2,1)S(1)} %bitcast.180, f32[12,512,1024]{2,1,0:T(8,128)} %get-tuple-element.88, f32[12,512]{1,0:T(8,128)S(1)} %fusion.11, f32[12,512]{1,0:T(8,128)S(1)} %get-tuple-element.87), kind=kOutput, calls=%fused_computation.151 | convolution fusion | flops 824573952 | bytes 27574272 | tf_op jit(solution)/shard_map/hqk,khe->qhe/dot_general | solution.py:146
  199.1 15.7 %fusion.162 = (f32[12,512]{1,0:T(8,128)S(1)}, f32[12,512,1024]{2,1,0:T(8,128)}) fusion(f32[512,1024,12]{1,0,2:T(8,128)} %copy.80, bf16[1024,12,64]{0,2,1:T(8,128)(2,1)S(1)} %bitcast.171, bf16[1,1024,12,64]{1,3,2,0:T(8,128)(2,1)S(1)} %bitcast.191, pred[512,1024]{1,0:T(8,128)(4,1)} %get-tuple-element.81), kind=kOutput, calls=%fused_computation.200 | convolution fusion | flops 824174592 | bytes 53239808 | tf_op jit(solution)/shard_map/qhe,khe->hqk/dot_general | solution.py:31
  214.8 11.0 %fusion.10 = f32[12,512]{1,0:T(8,128)S(1)} fusion(f32[12,512,1024]{2,1,0:T(8,128)} %get-tuple-element.90, f32[12,512]{1,0:T(8,128)S(1)} %get-tuple-element.89), kind=kLoop, calls=%fused_computation.26 | loop fusion | flops 12576768 | bytes 25214976 | tf_op jit(solution)/shard_map/reduce_sum | solution.py:142
  225.9 10.5 fusion.132
  245.1 44.4 %all_to_all.42 = bf16[4,320,768]{2,1,0:T(8,128)(2,1)S(1)} all-to-all(bf16[4,320,768]{2,1,0:T(8,128)(2,1)S(1)} %fusion.104), channel_id=1, replica_groups=mesh['replica'=8,'shard'=4] {'shard'}, dimensions={0} | all-to-all | bytes 3932160 | tf_op jit(solution)/shard_map/all_to_all | solution.py:171
  290.8 6.4 fusion.51
  297.3 9.6 fusion.70
  306.9 15.1 %copy.116 = bf16[1,1280,768]{2,0,1:T(2,128)(2,1)} copy(bf16[1,1280,768]{2,1,0:T(8,128)(2,1)S(1)} %fusion.70) | data formatting | bytes 3932160 | tf_op jit(solution)/shard_map/convert_element_type | solution.py:46
  322.5 13.7 %reduce.2 = bf16[1280,768]{1,0:T(8,128)(2,1)} reduce(bf16[1280,1,768]{2,1,0:T(2,128)(2,1)} %bitcast.174, bf16[]{:T(256)} %broadcast.378), dimensions={1}, to_apply=%bitcast.168.reduce_sub_computation | reduce | bytes 3932162
  340.2 4.5 all-to-all-start.1
  344.7 48.8 %all-gather = bf16[4,192,4]{1,2,0:T(4,128)(2,1)S(1)} all-gather(bf16[1,192,4]{1,2,0:T(4,128)(2,1)S(1)} %bitcast.216), channel_id=1, replica_groups=mesh['replica'=8,'shard'=4] {'shard'}, dimensions={0}, use_global_device_ids=true | all-gather | bytes 7680 | tf_op jit(solution)/shard_map/all_gather | solution.py:88
  398.1 4.8 reshape.409
  412.3 44.4 %all_to_all.43 = bf16[4,320,768]{2,1,0:T(8,128)(2,1)S(1)} all-to-all(bf16[4,320,768]{2,1,0:T(8,128)(2,1)S(1)} %fusion.107), channel_id=1, replica_groups=mesh['replica'=8,'shard'=4] {'shard'}, dimensions={0} | all-to-all | bytes 3932160 | tf_op jit(solution)/shard_map/all_to_all | solution.py:207
  458.0 10.0 convolution_bitcast_fusion
  468.1 19.0 %fusion.20 = bf16[1280,3072]{1,0:T(8,128)(2,1)S(1)} fusion(f32[1280,3072]{1,0:T(8,128)} %copy-done.54, bf16[1280,768]{1,0:T(8,128)(2,1)} %bitcast.197, bf16[1,3072,768]{2,1,0:T(8,128)(2,1)} %param.27), kind=kOutput, calls=%fused_computation.36 | convolution fusion | flops 6118440960 | bytes 30277632 | tf_op jit(solution)/shard_map/ecd,efd->ecf/dot_general | solution.py:51
  490.3 8.8 convolution_bitcast_fusion.1
  499.1 10.4 fusion.73
  509.5 15.3 %copy.115 = bf16[1,1280,768]{2,0,1:T(2,128)(2,1)} copy(bf16[1,1280,768]{2,1,0:T(8,128)(2,1)S(1)} %fusion.73) | data formatting | bytes 3932160 | tf_op jit(solution)/shard_map/convert_element_type | solution.py:61
  524.8 13.8 %reduce.3 = bf16[1280,768]{1,0:T(8,128)(2,1)} reduce(bf16[1280,1,768]{2,1,0:T(2,128)(2,1)} %bitcast.175, bf16[]{:T(256)} %broadcast.378), dimensions={1}, to_apply=%bitcast.167.reduce_sub_computation | reduce | bytes 3932162
  542.5 4.4 all-to-all-start.3
  550.7 39.7 %all-to-all-done.3 = bf16[4,2,122880]{2,1,0:T(2,128)(2,1)} async-done(((bf16[4,2,122880]{2,1,0:T(2,128)(2,1)}), bf16[4,2,122880]{2,1,0:T(2,128)(2,1)}, u32[]{:S(2)}, u32[]{:S(2)}) %all-to-all-start.3) | async-done | bytes 1966112 | tf_op jit(solution)/shard_map/all_to_all | solution.py:211
  590.4 5.1 reshape.411
  613.6 11.1 %fusion.21 = f32[12,64,1024]{2,1,0:T(8,128)S(1)} fusion(f32[12,512,1024]{2,1,0:T(8,128)} %get-tuple-element.88, f32[12,512]{1,0:T(8,128)S(1)} %log_add_fusion, bf16[1,1024,12,64]{1,3,2,0:T(8,128)(2,1)S(1)} %bitcast.186), kind=kOutput, calls=%fused_computation.38 | convolution fusion | flops 817889280 | bytes 29130752 | tf_op jit(solution)/shard_map/hqk,qhe->khe/dot_general | solution.py:246
  624.8 10.7 %add_convert_fusion = bf16[12,64,1024]{2,1,0:T(8,128)(2,1)S(1)} fusion(f32[12,64,1024]{2,1,0:T(8,128)S(1)} %fusion.21, f32[12,512,1024]{2,1,0:T(8,128)} %get-tuple-element.90, f32[12,512]{1,0:T(8,128)S(1)} %log_add_fusion.1, bf16[1,1024,12,64]{1,3,2,0:T(8,128)(2,1)S(1)} %bitcast.187), kind=kOutput, calls=%fused_computation.95 | convolution fusion | flops 819462144 | bytes 30703616 | tf_op jit(solution)/shard_map/hqk,qhe->khe/dot_general | solution.py:246
  639.5 16.2 %multiply_reduce_fusion = (f32[12,512]{1,0:T(8,128)S(1)}, f32[12,512,1024]{2,1,0:T(8,128)}) fusion(f32[12,512,1024]{2,1,0:T(8,128)} %get-tuple-element.88, f32[12,512]{1,0:T(8,128)S(1)} %log_add_fusion, bf16[1024,12,64]{0,2,1:T(8,128)(2,1)S(1)} %bitcast.182, bf16[1,1024,12,64]{1,3,2,0:T(8,128)(2,1)} %bitcast.188), kind=kOutput, calls=%fused_computation.15 | convolution fusion | flops 824174592 | bytes 52740096 | tf_op jit(solution)/shard_map/qhe,khe->hqk/dot_general | solution.py:252
  655.7 16.0 %multiply_reduce_fusion.1 = (f32[12,512]{1,0:T(8,128)S(1)}, f32[12,512,1024]{2,1,0:T(8,128)}) fusion(f32[12,512,1024]{2,1,0:T(8,128)} %get-tuple-element.90, f32[12,512]{1,0:T(8,128)S(1)} %log_add_fusion.1, bf16[1024,12,64]{0,2,1:T(8,128)(2,1)S(1)} %bitcast.183, bf16[1,1024,12,64]{1,3,2,0:T(8,128)(2,1)} %bitcast.189), kind=kOutput, calls=%fused_computation.18 | convolution fusion | flops 824174592 | bytes 52740096 | tf_op jit(solution)/shard_map/qhe,khe->hqk/dot_general | solution.py:252
  671.8 26.1 %subtract_multiply_fusion = f32[12,512,1024]{2,1,0:T(8,128)} fusion(f32[12,512,1024]{2,1,0:T(8,128)} %get-tuple-element.99, f32[12,512,1024]{2,1,0:T(8,128)} %get-tuple-element.88, f32[12,512]{1,0:T(8,128)S(1)} %get-tuple-element.98, f32[12,512]{1,0:T(8,128)S(1)} %log_add_fusion), kind=kLoop, calls=%fused_computation.14 | loop fusion | flops 18874368 | bytes 75546624 | tf_op jit(solution)/shard_map/mul | solution.py:256
  697.9 13.4 %fusion.126 = bf16[512,12,64]{0,2,1:T(8,128)(2,1)} fusion(bf16[1024,12,64]{0,2,1:T(8,128)(2,1)S(1)} %bitcast.172, f32[12,512,1024]{2,1,0:T(8,128)} %subtract_multiply_fusion), kind=kOutput, calls=%fused_computation.148 | convolution fusion | flops 811991040 | bytes 27525120 | tf_op jit(solution)/shard_map/hqk,khe->qhe/dot_general | solution.py:266
  711.3 26.0 %subtract_multiply_fusion.1 = f32[12,512,1024]{2,1,0:T(8,128)} fusion(f32[12,512,1024]{2,1,0:T(8,128)} %get-tuple-element.101, f32[12,512,1024]{2,1,0:T(8,128)} %get-tuple-element.90, f32[12,512]{1,0:T(8,128)S(1)} %get-tuple-element.100, f32[12,512]{1,0:T(8,128)S(1)} %log_add_fusion.1), kind=kLoop, calls=%fused_computation.17 | loop fusion | flops 18874368 | bytes 75546624 | tf_op jit(solution)/shard_map/mul | solution.py:256
  737.3 13.1 %fusion.129 = bf16[512,12,64]{0,2,1:T(8,128)(2,1)} fusion(bf16[1024,12,64]{0,2,1:T(8,128)(2,1)S(1)} %bitcast.173, f32[12,512,1024]{2,1,0:T(8,128)} %subtract_multiply_fusion.1), kind=kOutput, calls=%fused_computation.149 | convolution fusion | flops 811991040 | bytes 27525120 | tf_op jit(solution)/shard_map/hqk,khe->qhe/dot_general | solution.py:266
  756.0 10.9 %fusion.29 = f32[12,64,1024]{2,1,0:T(8,128)S(1)} fusion(f32[12,512,1024]{2,1,0:T(8,128)} %subtract_multiply_fusion, bf16[1,1024,12,64]{1,3,2,0:T(8,128)(2,1)S(1)} %bitcast.192), kind=kOutput, calls=%fused_computation.44 | convolution fusion | flops 811597824 | bytes 29097984 | tf_op jit(solution)/shard_map/hqk,qhe->khe/dot_general | solution.py:270
  766.9 10.7 %add_convert_fusion.1 = bf16[12,64,1024]{2,1,0:T(8,128)(2,1)S(1)} fusion(f32[12,64,1024]{2,1,0:T(8,128)S(1)} %fusion.29, f32[12,512,1024]{2,1,0:T(8,128)} %subtract_multiply_fusion.1, bf16[1,1024,12,64]{1,3,2,0:T(8,128)(2,1)S(1)} %bitcast.193), kind=kOutput, calls=%fused_computation.97 | convolution fusion | flops 813170688 | bytes 30670848 | tf_op jit(solution)/shard_map/hqk,qhe->khe/dot_general | solution.py:270
  785.4 31.0 %copy.94 = f32[12,512,1024]{1,0,2:T(8,128)} copy(f32[12,512,1024]{2,1,0:T(8,128)} %subtract_multiply_fusion) | data formatting | bytes 50331648 | tf_op jit(solution)/shard_map/mul | solution.py:256
  816.4 31.0 %copy.93 = f32[12,512,1024]{1,0,2:T(8,128)} copy(f32[12,512,1024]{2,1,0:T(8,128)} %subtract_multiply_fusion.1) | data formatting | bytes 50331648 | tf_op jit(solution)/shard_map/mul | solution.py:256
  862.5 38.0 %fusion.134 = f32[32,12]{1,0:T(8,128)S(1)} fusion(f32[12,512,1024]{1,0,2:T(8,128)} %copy.93, s32[512,1024]{0,1:T(8,128)S(1)} %copy-done.3), kind=kOutput, calls=%fused_computation.152 | convolution fusion | flops 2432696320 | bytes 27264512 | tf_op jit(solution)/shard_map/vsi,dsi->dv/dot_general | solution.py:257
  902.0 39.7 %fusion.136 = f32[32,12]{1,0:T(8,128)S(1)} fusion(f32[32,12]{1,0:T(8,128)S(1)} %fusion.134, f32[12,512,1024]{1,0,2:T(8,128)} %copy.94, s32[512,1024]{0,1:T(8,128)S(1)} %copy-done.1), kind=kOutput, calls=%fused_computation.154 | convolution fusion | flops 2432696832 | bytes 27266048 | tf_op jit(solution)/shard_map/vsi,dsi->dv/dot_general | solution.py:257
  941.8 17.0 %all-reduce.7 = (f32[768]{0:T(1024)S(1)}, f32[768]{0:T(1024)S(1)}, f32[32,12]{1,0:T(8,128)S(1)}) all-reduce(f32[768]{0:T(1024)S(1)} %get-tuple-element.62, f32[768]{0:T(1024)S(1)} %copy-done.47, f32[32,12]{1,0:T(8,128)S(1)} %fusion.136), channel_id=6, replica_groups=mesh['replica'=8,'shard'=4] {'shard'}, use_global_device_ids=true, to_apply=%region_26.27.clone | all-reduce | flops 1920 | bytes 15360
  958.9 22.7 %all-reduce.5 = (f32[192]{0:T(256)}, f32[192]{0:T(256)}, f32[192,4]{0,1:T(4,128)}, f32[8,12]{1,0:T(8,128)}) all-reduce(f32[192]{0:T(256)S(1)} %dynamic-slice.3, f32[192]{0:T(256)S(1)} %dynamic-slice.5, f32[192,4]{0,1:T(4,128)S(1)} %copy.108, ...), channel_id=1, replica_groups=mesh['replica'=8,'shard'=4] {'replica'}, use_global_device_ids=true, to_apply=%region_27.28 | all-reduce | flops 1248 | bytes 9984 | tf_op jit(solution)/shard_map/psum | solution.py:304
  981.6 60.0 %all-reduce.11.cloned.1.call-done = (f32[192,768]{1,0:T(8,128)}, f32[192,768]{1,0:T(8,128)}, f32[192,768]{1,0:T(8,128)}, f32[192,768]{1,0:T(8,128)}) async-done(((f32[192,768]{1,0:T(8,128)}, f32[192,768]{1,0:T(8,128)}, f32[192,768]{1,0:T(8,128)}, f32[192,768]{1,0:T(8,128)}), (f32[192,768]{1,0:T(8,128)}, f32[192,768]{1,0:T(8,128)}, f32[192,768]{1,0:T(8,128)}, ...) | async-done | bytes 2359312 | tf_op jit(solution)/shard_map/psum | solution.py:304
  1048.2 9.2 copy.129
  (255 shorter events, 133.8 us)
Async XLA Ops:
  7.2 142.4 %all-gather.10.cloned.1.call-start = ((), (), s32[]{:S(2)}) async-start(), calls=%async_computation.12 | async-start | bytes 1474560 | tf_op jit(solution)/shard_map/all_gather | solution.py:82
  7.9 145.6 %all-gather.12.cloned.1.call-start = ((), (), s32[]{:S(2)}) async-start(), calls=%async_computation.13 | async-start | bytes 1474560 | tf_op jit(solution)/shard_map/all_gather | solution.py:83
  8.7 175.6 %all-gather.8.cloned.1.call-start = ((), (), s32[]{:S(2)}) async-start(), calls=%async_computation.11 | async-start | bytes 1474560 | tf_op jit(solution)/shard_map/all_gather | solution.py:84
  9.4 228.3 %all-gather.14.cloned.1.call-start = ((), (), s32[]{:S(2)}) async-start(), calls=%async_computation.14 | async-start | bytes 1474560 | tf_op jit(solution)/shard_map/all_gather | solution.py:85
  27.3 157.0 %copy-start.40 = (f32[768]{0:T(1024)}, f32[768]{0:T(1024)S(1)}, u32[]{:S(2)}) copy-start(f32[768]{0:T(1024)S(1)} %convert_element_type.284) | copy-start | bytes 9220
  49.1 135.2 %copy-start.42 = (f32[1024]{0:T(1024)}, f32[1024]{0:T(1024)S(1)}, u32[]{:S(2)}) copy-start(f32[1024]{0:T(1024)S(1)} %fusion.146) | copy-start | bytes 12292
  51.2 49.7 %copy-start.2 = (s32[512,1024]{0,1:T(8,128)}, s32[512,1024]{0,1:T(8,128)S(1)}, u32[]{:S(2)}) copy-start(s32[512,1024]{0,1:T(8,128)S(1)} %fusion.84) | copy-start | bytes 6291460
  117.4 30.6 %copy-start.46 = (s32[1,1024]{1,0:T(1,128)S(1)}, s32[1,1024]{1,0:T(1,128)}, u32[]{:S(2)}) copy-start(s32[1,1024]{1,0:T(1,128)} %param.16) | copy-start | bytes 12292
  117.4 32.2 %copy-start.7 = (bf16[1024,768]{0,1:T(8,128)(2,1)S(1)}, bf16[1024,768]{0,1:T(8,128)(2,1)}, u32[]{:S(2)}) copy-start(bf16[1024,768]{0,1:T(8,128)(2,1)} %copy-done.6) | copy-start | bytes 4718596
  156.3 42.8 %copy-start.4 = (bf16[1024,768]{0,1:T(8,128)(2,1)}, bf16[1024,768]{0,1:T(8,128)(2,1)S(1)}, u32[]{:S(2)}) copy-start(bf16[1024,768]{0,1:T(8,128)(2,1)S(1)} %convolution_convert_fusion.1) | copy-start | bytes 4718596
  172.9 14.2 %copy-start.34 = (f32[12,512]{1,0:T(8,128)}, f32[12,512]{1,0:T(8,128)S(1)}, u32[]{:S(2)}) copy-start(f32[12,512]{1,0:T(8,128)S(1)} %get-tuple-element.87) | copy-start | bytes 73732
  187.1 12.0 %copy-start.12 = (bf16[1024,768]{0,1:T(8,128)(2,1)}, bf16[1024,768]{0,1:T(8,128)(2,1)S(1)}, u32[]{:S(2)}) copy-start(bf16[1024,768]{0,1:T(8,128)(2,1)S(1)} %convolution_convert_fusion.3) | copy-start | bytes 4718596
  187.1 12.0 %copy-start.21 = (bf16[1024,768]{0,1:T(8,128)(2,1)S(1)}, bf16[1024,768]{0,1:T(8,128)(2,1)}, u32[]{:S(2)}) copy-start(bf16[1024,768]{0,1:T(8,128)(2,1)} %convolution_convert_fusion.2) | copy-start | bytes 4718596
  214.8 11.0 %copy-start.13 = (bf16[1024,768]{0,1:T(8,128)(2,1)S(1)}, bf16[1024,768]{0,1:T(8,128)(2,1)}, u32[]{:S(2)}) copy-start(bf16[1024,768]{0,1:T(8,128)(2,1)} %copy-done.12) | copy-start | bytes 4718596
  225.9 10.5 copy-start.32
  237.7 53.1 %slice-start.5 = ((s8[4718592]{0:T(1024)(128)(4,1)}), s8[4194304]{0:T(1024)(128)(4,1)S(1)}, s32[]{:S(2)}) async-start(s8[4718592]{0:T(1024)(128)(4,1)} %bitcast.219), calls=%async_computation.30 | async-start | bytes 8388608
  242.4 48.4 %slice-start.6 = ((s8[4718592]{0:T(1024)(128)(4,1)}), s8[524288]{0:T(1024)(128)(4,1)S(1)}, s32[]{:S(2)}) async-start(s8[4718592]{0:T(1024)(128)(4,1)} %bitcast.219), calls=%async_computation.31 | async-start | bytes 1048576
  242.4 54.9 %slice-start.3 = ((s8[4718592]{0:T(1024)(128)(4,1)}), s8[4194304]{0:T(1024)(128)(4,1)S(1)}, s32[]{:S(2)}) async-start(s8[4718592]{0:T(1024)(128)(4,1)} %bitcast.217), calls=%async_computation.28 | async-start | bytes 8388608
  297.3 9.6 copy-start.54
  336.2 8.4 copy-start.50
  340.2 58.0 %all-to-all-start.1 = ((bf16[4,2,122880]{2,1,0:T(2,128)(2,1)}), bf16[4,2,122880]{2,1,0:T(2,128)(2,1)}, u32[]{:S(2)}, u32[]{:S(2)}) async-start(bf16[4,2,122880]{2,1,0:T(2,128)(2,1)} %reshape.408), calls=%async_computation.1 | async-start | bytes 3932160 | tf_op jit(solution)/shard_map/all_to_all | solution.py:175
  344.6 437.1 %reduce-scatter.20.cloned.1.call-start = ((), (), s32[]{:S(2)}) async-start(), calls=%async_computation.21 | async-start | bytes 10616832 | tf_op jit(solution)/shard_map/reduce_scatter | solution.py:319
  405.5 52.5 %slice-start.7 = ((s8[15728640]{0:T(1024)(128)(4,1)}), s8[4194304]{0:T(1024)(128)(4,1)S(1)}, s32[]{:S(2)}) async-start(s8[15728640]{0:T(1024)(128)(4,1)} %bitcast.221), calls=%async_computation.32 | async-start | bytes 8388608
  405.5 52.5 %slice-start.8 = ((s8[15728640]{0:T(1024)(128)(4,1)}), s8[4194304]{0:T(1024)(128)(4,1)S(1)}, s32[]{:S(2)}) async-start(s8[15728640]{0:T(1024)(128)(4,1)} %bitcast.221), calls=%async_computation.33 | async-start | bytes 8388608
  409.6 48.4 %slice-start.9 = ((s8[15728640]{0:T(1024)(128)(4,1)}), s8[4194304]{0:T(1024)(128)(4,1)S(1)}, s32[]{:S(2)}) async-start(s8[15728640]{0:T(1024)(128)(4,1)} %bitcast.221), calls=%async_computation.34 | async-start | bytes 8388608
  409.6 48.4 %slice-start.10 = ((s8[15728640]{0:T(1024)(128)(4,1)}), s8[3145728]{0:T(1024)(128)(4,1)S(1)}, s32[]{:S(2)}) async-start(s8[15728640]{0:T(1024)(128)(4,1)} %bitcast.221), calls=%async_computation.35 | async-start | bytes 6291456
  468.1 314.2 %reduce-scatter.18.cloned.1.call-start = ((), (), s32[]{:S(2)}) async-start(), calls=%async_computation.19 | async-start | bytes 10616832 | tf_op jit(solution)/shard_map/reduce_scatter | solution.py:318
  468.1 22.2 %copy-start.25 = (bf16[4,320,768]{2,1,0:T(8,128)(2,1)S(1)}, bf16[4,320,768]{2,1,0:T(8,128)(2,1)}, u32[]{:S(2)}) copy-start(bf16[4,320,768]{2,1,0:T(8,128)(2,1)} %copy-done.24) | copy-start | bytes 5898244
  538.6 8.4 copy-start.38
  542.5 47.9 %all-to-all-start.3 = ((bf16[4,2,122880]{2,1,0:T(2,128)(2,1)}), bf16[4,2,122880]{2,1,0:T(2,128)(2,1)}, u32[]{:S(2)}, u32[]{:S(2)}) async-start(bf16[4,2,122880]{2,1,0:T(2,128)(2,1)} %reshape.410), calls=%async_computation.3 | async-start | bytes 3932160 | tf_op jit(solution)/shard_map/all_to_all | solution.py:211
  546.9 237.4 %reduce-scatter.22.cloned.1.call-start = ((), (), s32[]{:S(2)}) async-start(), calls=%async_computation.23 | async-start | bytes 491520
  550.6 349.8 %reduce-scatter.16.cloned.1.call-start = ((), (), s32[]{:S(2)}) async-start(), calls=%async_computation.18 | async-start | bytes 2949120 | tf_op jit(solution)/shard_map/reduce_scatter | solution.py:298
  610.2 290.2 %reduce-scatter.14.cloned.1.call-start = ((), (), s32[]{:S(2)}) async-start(), calls=%async_computation.17 | async-start | bytes 2949120 | tf_op jit(solution)/shard_map/reduce_scatter | solution.py:297
  613.6 11.2 %copy-start.20 = (bf16[1024,768]{0,1:T(8,128)(2,1)}, bf16[1024,768]{0,1:T(8,128)(2,1)S(1)}, u32[]{:S(2)}) copy-start(bf16[1024,768]{0,1:T(8,128)(2,1)S(1)} %convolution_convert_fusion) | copy-start | bytes 4718596
  624.8 11.9 %copy-start.8 = (bf16[1024,768]{0,1:T(8,128)(2,1)S(1)}, bf16[1024,768]{0,1:T(8,128)(2,1)}, u32[]{:S(2)}) copy-start(bf16[1024,768]{0,1:T(8,128)(2,1)} %copy-done.6) | copy-start | bytes 4718596
  624.8 11.9 %copy-start.41 = (f32[768]{0:T(1024)S(1)}, f32[768]{0:T(1024)}, u32[]{:S(2)}) copy-start(f32[768]{0:T(1024)} %copy-done.40) | copy-start | bytes 9220
  624.8 11.9 %copy-start.43 = (f32[1024]{0:T(1024)S(1)}, f32[1024]{0:T(1024)}, u32[]{:S(2)}) copy-start(f32[1024]{0:T(1024)} %copy-done.42) | copy-start | bytes 12292
  671.7 228.8 %reduce-scatter.10.cloned.1.call-start = ((), (), s32[]{:S(2)}) async-start(), calls=%async_computation.15 | async-start | bytes 2949120 | tf_op jit(solution)/shard_map/reduce_scatter | solution.py:295
  671.8 26.1 %copy-start.5 = (bf16[1024,768]{0,1:T(8,128)(2,1)S(1)}, bf16[1024,768]{0,1:T(8,128)(2,1)}, u32[]{:S(2)}) copy-start(bf16[1024,768]{0,1:T(8,128)(2,1)} %copy-done.4) | copy-start | bytes 4718596
  756.0 144.6 %reduce-scatter.12.cloned.1.call-start = ((), (), s32[]{:S(2)}) async-start(), calls=%async_computation.16 | async-start | bytes 2949120 | tf_op jit(solution)/shard_map/reduce_scatter | solution.py:296
  781.7 199.9 %all-gather.18.cloned.1.call-start = ((), (), s32[]{:S(2)}) async-start(), calls=%async_computation.22 | async-start | bytes 10616832 | tf_op jit(solution)/shard_map/all_gather | solution.py:323
  782.3 199.3 %all-gather.16.cloned.1.call-start = ((), (), s32[]{:S(2)}) async-start(), calls=%async_computation.20 | async-start | bytes 10616832 | tf_op jit(solution)/shard_map/all_gather | solution.py:322
  783.0 258.6 %all-reduce.11.cloned.1.call-start = ((), (), s32[]{:S(2)}) async-start(), calls=%async_computation.24 | async-start | bytes 4718592 | tf_op jit(solution)/shard_map/psum | solution.py:304
  816.4 31.0 %copy-start.17 = (bf16[1024,768]{0,1:T(8,128)(2,1)S(1)}, bf16[1024,768]{0,1:T(8,128)(2,1)}, u32[]{:S(2)}) copy-start(bf16[1024,768]{0,1:T(8,128)(2,1)} %get-tuple-element.80) | copy-start | bytes 4718596
  902.0 39.7 %copy-start.47 = (f32[768]{0:T(1024)S(1)}, f32[768]{0:T(1024)}, u32[]{:S(2)}) copy-start(f32[768]{0:T(1024)} %get-tuple-element.60) | copy-start | bytes 9220
  1047.4 10.0 slice-start
  1048.2 9.2 slice-start.1
  1048.2 9.2 slice-start.2
  (34 other events, 90.4 us)
Sparse Core Ops, SparseCore 0:
  9.6 33.3 all-gather.9
  44.5 29.5 all-gather.11
  75.7 29.5 all-gather.7
  106.7 29.5 all-gather.13
  468.2 75.7 reduce-scatter.19
  547.9 76.4 reduce-scatter.17
  627.3 20.5 reduce-scatter.21
  650.3 46.2 reduce-scatter.15
  699.1 47.5 reduce-scatter.13
  756.1 47.1 reduce-scatter.9
  805.7 47.5 reduce-scatter.11
  855.2 58.3 all-gather.17
  915.6 58.7 all-gather.15
  978.2 63.3 all-reduce.10
where the time goes:
time: 1080 us; the launch traced here: 1070 us
  matrix products  387 us (36%)
  local copies, waits for them, and re-layouts  227 us (21%)
  blocking collectives  203 us (19%)
  other arithmetic  121 us (11%)
  waiting for transfers between devices  104 us (10%)
  between operations  17.2 us (2%)
    dot_general x2, matrix products, on_device(): jnp.einsum('vsi,dsi->dv', grad_scores, matches.astype(jnp.float32), preci...  77.7 us
    unnamed x159, local copies, waits for them, and re-layouts  73 us
    mul x2, local copies, waits for them, and re-layouts, on_device(): grad_scores = chances * (grad_chances - inner_sum)  62 us
    dot_general x2, local copies, waits for them, and re-layouts, block_scores(): jnp.einsum('rni,rf->fni', slot_indicators, relative_bias_table, preferred...  60.5 us
    psum x1, waiting for transfers between devices, on_device(): lax.psum((owned_grads[0], owned_grads[1], owned_grads[2], owned_grads[3],...  60 us
    mul x2, other arithmetic, on_device(): grad_scores = chances * (grad_chances - inner_sum)  52 us
    all_gather x1, blocking collectives, on_device(): lax.all_gather(w_router, 'shard', axis=0, tiled=True)  48.8 us
    all_to_all x1, blocking collectives, on_device(): lax.all_to_all(outgoing, 'shard', split_axis=0, concat_axis=1, tiled=True)  44.4 us
  transfers between devices with their start and end apart: 16, of which 2 were waited for; matrix products, arithmetic and copies ran while one was open for 58% of the time, Pallas kernels for 0%

commit v1 on v0

--- a/solution.py
+++ b/solution.py
@@ -159,7 +159,11 @@
     chosen = (routes == jnp.arange(experts, dtype=jnp.int32)[None, :]).astype(jnp.int32)
     chosen_f = chosen.astype(jnp.float32)
     chosen_gate = jnp.sum(gate_probs * chosen_f, axis=-1)
-    slot_index = jnp.cumsum(chosen, axis=0) - chosen
+    row_ids = jnp.arange(row_count, dtype=jnp.int32)
+    earlier = (row_ids[None, :] < row_ids[:, None]).astype(jnp.bfloat16)
+    slot_index = jnp.dot(
+        earlier, chosen.astype(jnp.bfloat16), preferred_element_type=jnp.float32
+    ).astype(jnp.int32)
     capacity = 5 * row_count // (4 * experts)
     slot_range = jnp.arange(capacity, dtype=jnp.int32)
     places = (

time: 1080 us -> 1080 us (level)
    unnamed x159 -> x161, local copies, waits for them, and re-layouts: 73 us -> 71.4 us
    unnamed x7 -> x6, other arithmetic: 27.6 us -> 27.5 us
where the time goes in v1:
time: 1080 us; the launch traced here: 1070 us
  matrix products  388 us (36%)
  local copies, waits for them, and re-layouts  225 us (21%)
  blocking collectives  203 us (19%)
  other arithmetic  118 us (11%)
  waiting for transfers between devices  104 us (10%)
  between operations  17.2 us (2%)
    dot_general x2, matrix products, on_device(): jnp.einsum('vsi,dsi->dv', grad_scores, matches.astype(jnp.float32), preci...  77.7 us
    unnamed x161, local copies, waits for them, and re-layouts  71.4 us
    mul x2, local copies, waits for them, and re-layouts, on_device(): grad_scores = chances * (grad_chances - inner_sum)  62 us
    dot_general x2, local copies, waits for them, and re-layouts, block_scores(): jnp.einsum('rni,rf->fni', slot_indicators, relative_bias_table, preferred...  61.1 us
    psum x1, waiting for transfers between devices, on_device(): lax.psum((owned_grads[0], owned_grads[1], owned_grads[2], owned_grads[3],...  60 us
    mul x2, other arithmetic, on_device(): grad_scores = chances * (grad_chances - inner_sum)  52 us
    all_gather x1, blocking collectives, on_device(): lax.all_gather(w_router, 'shard', axis=0, tiled=True)  48.8 us
    all_to_all x1, blocking collectives, on_device(): lax.all_to_all(grad_slots, 'shard', split_axis=0, concat_axis=1, tiled=True)  44.4 us
  transfers between devices with their start and end apart: 16, of which 2 were waited for; matrix products, arithmetic and copies ran while one was open for 58% of the time, Pallas kernels for 0%

profile of v1, /device:TPU:0, one launch (start us, length us, event | category | flops | bytes accessed | tf_op | source)
XLA Modules:
  0.0 1065.1 jit_solution(12687554596998797300)
XLA Ops:
  16.7 13.6 %all-reduce.8 = (bf16[768]{0:T(1024)(128)(2,1)S(1)}, bf16[768]{0:T(1024)(128)(2,1)S(1)}) all-reduce(bf16[768]{0:T(1024)(128)(2,1)S(1)} %dynamic-update-slice, bf16[768]{0:T(1024)(128)(2,1)S(1)} %dynamic-update-slice.1), channel_id=1, replica_groups=mesh['replica'=8,'shard'=4] {'shard'}, use_global_device_ids=true, to_apply=%add | all-reduce | flops 1536 | bytes 6144
  31.6 12.1 %all_gather.42 = bf16[32,12]{1,0:T(8,128)(2,1)S(1)} all-gather(bf16[8,12]{1,0:T(8,128)(2,1)} %param.25), channel_id=1, replica_groups=mesh['replica'=8,'shard'=4] {'shard'}, dimensions={0}, use_global_device_ids=true | all-gather | bytes 960 | tf_op jit(solution)/shard_map/all_gather | solution.py:89
  51.1 16.3 %fusion.1 = f32[512,1024,12]{0,2,1:T(8,128)} fusion(s32[512,1024]{0,1:T(8,128)S(1)} %fusion.86, bf16[32,12]{1,0:T(8,128)(2,1)S(1)} %all_gather.42), kind=kOutput, calls=%fused_computation.2 | convolution fusion | flops 419430400 | bytes 27263744 | tf_op jit(solution)/shard_map/rni,rf->fni/dot_general | solution.py:32
  67.4 30.5 %copy.81 = f32[512,1024,12]{1,0,2:T(8,128)} copy(f32[512,1024,12]{0,2,1:T(8,128)} %fusion.1) | data formatting | bytes 50331648 | tf_op jit(solution)/shard_map/rni,rf->fni/dot_general | solution.py:32
  98.0 16.5 %fusion.3 = f32[512,1024,12]{0,2,1:T(8,128)} fusion(s32[512,1024]{0,1:T(8,128)S(1)} %fusion.85, bf16[32,12]{1,0:T(8,128)(2,1)S(1)} %all_gather.42), kind=kOutput, calls=%fused_computation.5 | convolution fusion | flops 419430400 | bytes 27263744 | tf_op jit(solution)/shard_map/rni,rf->fni/dot_general | solution.py:32
  114.5 30.6 %copy.80 = f32[512,1024,12]{1,0,2:T(8,128)} copy(f32[512,1024,12]{0,2,1:T(8,128)} %fusion.3) | data formatting | bytes 50331648 | tf_op jit(solution)/shard_map/rni,rf->fni/dot_general | solution.py:32
  153.4 16.6 %fusion.173 = (f32[12,512]{1,0:T(8,128)S(1)}, f32[12,512,1024]{2,1,0:T(8,128)}) fusion(f32[512,1024,12]{1,0,2:T(8,128)} %copy.81, bf16[1024,12,64]{0,2,1:T(8,128)(2,1)S(1)} %bitcast.164, bf16[1,1024,12,64]{1,3,2,0:T(8,128)(2,1)} %bitcast.184, pred[512,1024]{1,0:T(8,128)(4,1)} %get-tuple-element.82), kind=kOutput, calls=%fused_computation.204 | convolution fusion | flops 824174592 | bytes 53239808 | tf_op jit(solution)/shard_map/qhe,khe->hqk/dot_general | solution.py:31
  170.0 11.4 %fusion.11 = f32[12,512]{1,0:T(8,128)S(1)} fusion(f32[12,512,1024]{2,1,0:T(8,128)} %get-tuple-element.88, f32[12,512]{1,0:T(8,128)S(1)} %get-tuple-element.87), kind=kLoop, calls=%fused_computation.27 | loop fusion | flops 12576768 | bytes 25214976 | tf_op jit(solution)/shard_map/reduce_sum | solution.py:142
  184.3 12.0 %fusion.134 = bf16[512,12,64]{0,2,1:T(8,128)(2,1)} fusion(bf16[1024,12,64]{0,2,1:T(8,128)(2,1)S(1)} %bitcast.174, f32[12,512,1024]{2,1,0:T(8,128)} %get-tuple-element.88, f32[12,512]{1,0:T(8,128)S(1)} %fusion.11, f32[12,512]{1,0:T(8,128)S(1)} %get-tuple-element.87), kind=kOutput, calls=%fused_computation.153 | convolution fusion | flops 824573952 | bytes 27574272 | tf_op jit(solution)/shard_map/hqk,khe->qhe/dot_general | solution.py:146
  196.3 15.8 %fusion.174 = (f32[12,512]{1,0:T(8,128)S(1)}, f32[12,512,1024]{2,1,0:T(8,128)}) fusion(f32[512,1024,12]{1,0,2:T(8,128)} %copy.80, bf16[1024,12,64]{0,2,1:T(8,128)(2,1)S(1)} %bitcast.165, bf16[1,1024,12,64]{1,3,2,0:T(8,128)(2,1)S(1)} %bitcast.185, pred[512,1024]{1,0:T(8,128)(4,1)} %get-tuple-element.81), kind=kOutput, calls=%fused_computation.205 | convolution fusion | flops 824174592 | bytes 53239808 | tf_op jit(solution)/shard_map/qhe,khe->hqk/dot_general | solution.py:31
  212.1 11.0 %fusion.10 = f32[12,512]{1,0:T(8,128)S(1)} fusion(f32[12,512,1024]{2,1,0:T(8,128)} %get-tuple-element.90, f32[12,512]{1,0:T(8,128)S(1)} %get-tuple-element.89), kind=kLoop, calls=%fused_computation.26 | loop fusion | flops 12576768 | bytes 25214976 | tf_op jit(solution)/shard_map/reduce_sum | solution.py:142
  223.1 10.5 fusion.133
  242.3 44.2 %all_to_all.42 = bf16[4,320,768]{2,1,0:T(8,128)(2,1)S(1)} all-to-all(bf16[4,320,768]{2,1,0:T(8,128)(2,1)S(1)} %fusion.105), channel_id=1, replica_groups=mesh['replica'=8,'shard'=4] {'shard'}, dimensions={0} | all-to-all | bytes 3932160 | tf_op jit(solution)/shard_map/all_to_all | solution.py:175
  287.8 6.4 fusion.51
  294.3 9.6 fusion.71
  304.0 15.1 %copy.114 = bf16[1,1280,768]{2,0,1:T(2,128)(2,1)} copy(bf16[1,1280,768]{2,1,0:T(8,128)(2,1)S(1)} %fusion.71) | data formatting | bytes 3932160 | tf_op jit(solution)/shard_map/convert_element_type | solution.py:46
  319.5 13.7 %reduce = bf16[1280,768]{1,0:T(8,128)(2,1)} reduce(bf16[1280,1,768]{2,1,0:T(2,128)(2,1)} %bitcast.168, bf16[]{:T(256)} %broadcast.362), dimensions={1}, to_apply=%bitcast.163.reduce_sub_computation | reduce | bytes 3932162
  337.2 4.5 all-to-all-start.1
  341.7 48.8 %all-gather = bf16[4,192,4]{1,2,0:T(4,128)(2,1)S(1)} all-gather(bf16[1,192,4]{1,2,0:T(4,128)(2,1)S(1)} %bitcast.208), channel_id=1, replica_groups=mesh['replica'=8,'shard'=4] {'shard'}, dimensions={0}, use_global_device_ids=true | all-gather | bytes 7680 | tf_op jit(solution)/shard_map/all_gather | solution.py:88
  395.1 4.8 reshape.391
  409.3 44.4 %all_to_all.43 = bf16[4,320,768]{2,1,0:T(8,128)(2,1)S(1)} all-to-all(bf16[4,320,768]{2,1,0:T(8,128)(2,1)S(1)} %fusion.108), channel_id=1, replica_groups=mesh['replica'=8,'shard'=4] {'shard'}, dimensions={0} | all-to-all | bytes 3932160 | tf_op jit(solution)/shard_map/all_to_all | solution.py:211
  455.0 10.0 convolution_bitcast_fusion
  465.1 19.0 %fusion.20 = bf16[1280,3072]{1,0:T(8,128)(2,1)S(1)} fusion(f32[1280,3072]{1,0:T(8,128)} %copy-done.54, bf16[1280,768]{1,0:T(8,128)(2,1)} %bitcast.191, bf16[1,3072,768]{2,1,0:T(8,128)(2,1)} %param.27), kind=kOutput, calls=%fused_computation.36 | convolution fusion | flops 6118440960 | bytes 30277632 | tf_op jit(solution)/shard_map/ecd,efd->ecf/dot_general | solution.py:51
  487.3 8.8 convolution_bitcast_fusion.1
  496.1 10.4 fusion.74
  506.5 15.3 %copy.113 = bf16[1,1280,768]{2,0,1:T(2,128)(2,1)} copy(bf16[1,1280,768]{2,1,0:T(8,128)(2,1)S(1)} %fusion.74) | data formatting | bytes 3932160 | tf_op jit(solution)/shard_map/convert_element_type | solution.py:61
  521.8 13.8 %reduce.1 = bf16[1280,768]{1,0:T(8,128)(2,1)} reduce(bf16[1280,1,768]{2,1,0:T(2,128)(2,1)} %bitcast.169, bf16[]{:T(256)} %broadcast.362), dimensions={1}, to_apply=%bitcast.162.reduce_sub_computation | reduce | bytes 3932162
  539.5 4.4 all-to-all-start.3
  547.6 39.8 %all-to-all-done.3 = bf16[4,2,122880]{2,1,0:T(2,128)(2,1)} async-done(((bf16[4,2,122880]{2,1,0:T(2,128)(2,1)}), bf16[4,2,122880]{2,1,0:T(2,128)(2,1)}, u32[]{:S(2)}, u32[]{:S(2)}) %all-to-all-start.3) | async-done | bytes 1966112 | tf_op jit(solution)/shard_map/all_to_all | solution.py:215
  587.4 5.1 reshape.393
  610.6 11.1 %fusion.21 = f32[12,64,1024]{2,1,0:T(8,128)S(1)} fusion(f32[12,512,1024]{2,1,0:T(8,128)} %get-tuple-element.88, f32[12,512]{1,0:T(8,128)S(1)} %log_add_fusion, bf16[1,1024,12,64]{1,3,2,0:T(8,128)(2,1)S(1)} %bitcast.180), kind=kOutput, calls=%fused_computation.38 | convolution fusion | flops 817889280 | bytes 29130752 | tf_op jit(solution)/shard_map/hqk,qhe->khe/dot_general | solution.py:250
  621.8 10.7 %add_convert_fusion = bf16[12,64,1024]{2,1,0:T(8,128)(2,1)S(1)} fusion(f32[12,64,1024]{2,1,0:T(8,128)S(1)} %fusion.21, f32[12,512,1024]{2,1,0:T(8,128)} %get-tuple-element.90, f32[12,512]{1,0:T(8,128)S(1)} %log_add_fusion.1, bf16[1,1024,12,64]{1,3,2,0:T(8,128)(2,1)S(1)} %bitcast.181), kind=kOutput, calls=%fused_computation.97 | convolution fusion | flops 819462144 | bytes 30703616 | tf_op jit(solution)/shard_map/hqk,qhe->khe/dot_general | solution.py:250
  636.6 16.2 %multiply_reduce_fusion = (f32[12,512]{1,0:T(8,128)S(1)}, f32[12,512,1024]{2,1,0:T(8,128)}) fusion(f32[12,512,1024]{2,1,0:T(8,128)} %get-tuple-element.88, f32[12,512]{1,0:T(8,128)S(1)} %log_add_fusion, bf16[1024,12,64]{0,2,1:T(8,128)(2,1)S(1)} %bitcast.176, bf16[1,1024,12,64]{1,3,2,0:T(8,128)(2,1)} %bitcast.182), kind=kOutput, calls=%fused_computation.15 | convolution fusion | flops 824174592 | bytes 52740096 | tf_op jit(solution)/shard_map/qhe,khe->hqk/dot_general | solution.py:256
  652.7 16.0 %multiply_reduce_fusion.1 = (f32[12,512]{1,0:T(8,128)S(1)}, f32[12,512,1024]{2,1,0:T(8,128)}) fusion(f32[12,512,1024]{2,1,0:T(8,128)} %get-tuple-element.90, f32[12,512]{1,0:T(8,128)S(1)} %log_add_fusion.1, bf16[1024,12,64]{0,2,1:T(8,128)(2,1)S(1)} %bitcast.177, bf16[1,1024,12,64]{1,3,2,0:T(8,128)(2,1)} %bitcast.183), kind=kOutput, calls=%fused_computation.18 | convolution fusion | flops 824174592 | bytes 52740096 | tf_op jit(solution)/shard_map/qhe,khe->hqk/dot_general | solution.py:256
  668.8 26.1 %subtract_multiply_fusion = f32[12,512,1024]{2,1,0:T(8,128)} fusion(f32[12,512,1024]{2,1,0:T(8,128)} %get-tuple-element.99, f32[12,512,1024]{2,1,0:T(8,128)} %get-tuple-element.88, f32[12,512]{1,0:T(8,128)S(1)} %get-tuple-element.98, f32[12,512]{1,0:T(8,128)S(1)} %log_add_fusion), kind=kLoop, calls=%fused_computation.14 | loop fusion | flops 18874368 | bytes 75546624 | tf_op jit(solution)/shard_map/mul | solution.py:260
  694.9 13.4 %fusion.127 = bf16[512,12,64]{0,2,1:T(8,128)(2,1)} fusion(bf16[1024,12,64]{0,2,1:T(8,128)(2,1)S(1)} %bitcast.166, f32[12,512,1024]{2,1,0:T(8,128)} %subtract_multiply_fusion), kind=kOutput, calls=%fused_computation.150 | convolution fusion | flops 811991040 | bytes 27525120 | tf_op jit(solution)/shard_map/hqk,khe->qhe/dot_general | solution.py:270
  708.3 25.9 %subtract_multiply_fusion.1 = f32[12,512,1024]{2,1,0:T(8,128)} fusion(f32[12,512,1024]{2,1,0:T(8,128)} %get-tuple-element.101, f32[12,512,1024]{2,1,0:T(8,128)} %get-tuple-element.90, f32[12,512]{1,0:T(8,128)S(1)} %get-tuple-element.100, f32[12,512]{1,0:T(8,128)S(1)} %log_add_fusion.1), kind=kLoop, calls=%fused_computation.17 | loop fusion | flops 18874368 | bytes 75546624 | tf_op jit(solution)/shard_map/mul | solution.py:260
  734.2 13.1 %fusion.130 = bf16[512,12,64]{0,2,1:T(8,128)(2,1)} fusion(bf16[1024,12,64]{0,2,1:T(8,128)(2,1)S(1)} %bitcast.167, f32[12,512,1024]{2,1,0:T(8,128)} %subtract_multiply_fusion.1), kind=kOutput, calls=%fused_computation.151 | convolution fusion | flops 811991040 | bytes 27525120 | tf_op jit(solution)/shard_map/hqk,khe->qhe/dot_general | solution.py:270
  752.9 10.9 %fusion.29 = f32[12,64,1024]{2,1,0:T(8,128)S(1)} fusion(f32[12,512,1024]{2,1,0:T(8,128)} %subtract_multiply_fusion, bf16[1,1024,12,64]{1,3,2,0:T(8,128)(2,1)S(1)} %bitcast.186), kind=kOutput, calls=%fused_computation.44 | convolution fusion | flops 811597824 | bytes 29097984 | tf_op jit(solution)/shard_map/hqk,qhe->khe/dot_general | solution.py:274
  763.9 10.7 %add_convert_fusion.1 = bf16[12,64,1024]{2,1,0:T(8,128)(2,1)S(1)} fusion(f32[12,64,1024]{2,1,0:T(8,128)S(1)} %fusion.29, f32[12,512,1024]{2,1,0:T(8,128)} %subtract_multiply_fusion.1, bf16[1,1024,12,64]{1,3,2,0:T(8,128)(2,1)S(1)} %bitcast.187), kind=kOutput, calls=%fused_computation.99 | convolution fusion | flops 813170688 | bytes 30670848 | tf_op jit(solution)/shard_map/hqk,qhe->khe/dot_general | solution.py:274
  782.3 31.0 %copy.94 = f32[12,512,1024]{1,0,2:T(8,128)} copy(f32[12,512,1024]{2,1,0:T(8,128)} %subtract_multiply_fusion) | data formatting | bytes 50331648 | tf_op jit(solution)/shard_map/mul | solution.py:260
  813.3 30.9 %copy.93 = f32[12,512,1024]{1,0,2:T(8,128)} copy(f32[12,512,1024]{2,1,0:T(8,128)} %subtract_multiply_fusion.1) | data formatting | bytes 50331648 | tf_op jit(solution)/shard_map/mul | solution.py:260
  859.4 37.9 %fusion.136 = f32[32,12]{1,0:T(8,128)S(1)} fusion(f32[12,512,1024]{1,0,2:T(8,128)} %copy.93, s32[512,1024]{0,1:T(8,128)S(1)} %copy-done.3), kind=kOutput, calls=%fused_computation.155 | convolution fusion | flops 2432696320 | bytes 27264512 | tf_op jit(solution)/shard_map/vsi,dsi->dv/dot_general | solution.py:261
  898.9 39.7 %fusion.138 = f32[32,12]{1,0:T(8,128)S(1)} fusion(f32[32,12]{1,0:T(8,128)S(1)} %fusion.136, f32[12,512,1024]{1,0,2:T(8,128)} %copy.94, s32[512,1024]{0,1:T(8,128)S(1)} %copy-done.1), kind=kOutput, calls=%fused_computation.157 | convolution fusion | flops 2432696832 | bytes 27266048 | tf_op jit(solution)/shard_map/vsi,dsi->dv/dot_general | solution.py:261
  938.7 16.9 %all-reduce.7 = (f32[768]{0:T(1024)S(1)}, f32[768]{0:T(1024)S(1)}, f32[32,12]{1,0:T(8,128)S(1)}) all-reduce(f32[768]{0:T(1024)S(1)} %get-tuple-element.62, f32[768]{0:T(1024)S(1)} %copy-done.48, f32[32,12]{1,0:T(8,128)S(1)} %fusion.138), channel_id=6, replica_groups=mesh['replica'=8,'shard'=4] {'shard'}, use_global_device_ids=true, to_apply=%region_24.25.clone | all-reduce | flops 1920 | bytes 15360
  955.7 22.8 %all-reduce.5 = (f32[192]{0:T(256)}, f32[192]{0:T(256)}, f32[192,4]{0,1:T(4,128)}, f32[8,12]{1,0:T(8,128)}) all-reduce(f32[192]{0:T(256)S(1)} %dynamic-slice.3, f32[192]{0:T(256)S(1)} %dynamic-slice.5, f32[192,4]{0,1:T(4,128)S(1)} %copy.108, ...), channel_id=1, replica_groups=mesh['replica'=8,'shard'=4] {'replica'}, use_global_device_ids=true, to_apply=%region_25.26 | all-reduce | flops 1248 | bytes 9984 | tf_op jit(solution)/shard_map/psum | solution.py:308
  978.5 60.0 %all-reduce.11.cloned.1.call-done = (f32[192,768]{1,0:T(8,128)}, f32[192,768]{1,0:T(8,128)}, f32[192,768]{1,0:T(8,128)}, f32[192,768]{1,0:T(8,128)}) async-done(((f32[192,768]{1,0:T(8,128)}, f32[192,768]{1,0:T(8,128)}, f32[192,768]{1,0:T(8,128)}, f32[192,768]{1,0:T(8,128)}), (f32[192,768]{1,0:T(8,128)}, f32[192,768]{1,0:T(8,128)}, f32[192,768]{1,0:T(8,128)}, ...) | async-done | bytes 2359312 | tf_op jit(solution)/shard_map/psum | solution.py:308
  1045.1 9.2 copy.127
  (252 shorter events, 130.4 us)
Async XLA Ops:
  7.2 36.5 %copy-start.27 = (bf16[1024,768]{1,0:T(8,128)(2,1)S(1)}, bf16[1024,768]{1,0:T(8,128)(2,1)}, u32[]{:S(2)}) copy-start(bf16[1024,768]{1,0:T(8,128)(2,1)} %param.14) | copy-start | bytes 4718596
  7.2 139.5 %all-gather.10.cloned.1.call-start = ((), (), s32[]{:S(2)}) async-start(), calls=%async_computation.12 | async-start | bytes 1474560 | tf_op jit(solution)/shard_map/all_gather | solution.py:82
  7.9 142.7 %all-gather.12.cloned.1.call-start = ((), (), s32[]{:S(2)}) async-start(), calls=%async_computation.13 | async-start | bytes 1474560 | tf_op jit(solution)/shard_map/all_gather | solution.py:83
  8.7 172.8 %all-gather.8.cloned.1.call-start = ((), (), s32[]{:S(2)}) async-start(), calls=%async_computation.11 | async-start | bytes 1474560 | tf_op jit(solution)/shard_map/all_gather | solution.py:84
  9.4 225.6 %all-gather.14.cloned.1.call-start = ((), (), s32[]{:S(2)}) async-start(), calls=%async_computation.14 | async-start | bytes 1474560 | tf_op jit(solution)/shard_map/all_gather | solution.py:85
  30.3 151.1 %copy-start.41 = (f32[768]{0:T(1024)}, f32[768]{0:T(1024)S(1)}, u32[]{:S(2)}) copy-start(f32[768]{0:T(1024)S(1)} %convert_element_type.287) | copy-start | bytes 9220
  45.6 21.8 %copy-start.45 = (f32[1024]{0:T(1024)}, f32[1024]{0:T(1024)S(1)}, u32[]{:S(2)}) copy-start(f32[1024]{0:T(1024)S(1)} %fusion.67) | copy-start | bytes 12292
  45.6 135.9 %copy-start.43 = (f32[1024]{0:T(1024)}, f32[1024]{0:T(1024)S(1)}, u32[]{:S(2)}) copy-start(f32[1024]{0:T(1024)S(1)} %fusion.156) | copy-start | bytes 12292
  47.7 50.3 %copy-start.2 = (s32[512,1024]{0,1:T(8,128)}, s32[512,1024]{0,1:T(8,128)S(1)}, u32[]{:S(2)}) copy-start(s32[512,1024]{0,1:T(8,128)S(1)} %fusion.85) | copy-start | bytes 6291460
  114.5 30.6 %copy-start.47 = (s32[1,1024]{1,0:T(1,128)S(1)}, s32[1,1024]{1,0:T(1,128)}, u32[]{:S(2)}) copy-start(s32[1,1024]{1,0:T(1,128)} %param.16) | copy-start | bytes 12292
  114.5 32.2 %copy-start.7 = (bf16[1024,768]{0,1:T(8,128)(2,1)S(1)}, bf16[1024,768]{0,1:T(8,128)(2,1)}, u32[]{:S(2)}) copy-start(bf16[1024,768]{0,1:T(8,128)(2,1)} %copy-done.6) | copy-start | bytes 4718596
  153.4 42.9 %copy-start.4 = (bf16[1024,768]{0,1:T(8,128)(2,1)}, bf16[1024,768]{0,1:T(8,128)(2,1)S(1)}, u32[]{:S(2)}) copy-start(bf16[1024,768]{0,1:T(8,128)(2,1)S(1)} %convolution_convert_fusion.1) | copy-start | bytes 4718596
  170.0 14.2 %copy-start.35 = (f32[12,512]{1,0:T(8,128)}, f32[12,512]{1,0:T(8,128)S(1)}, u32[]{:S(2)}) copy-start(f32[12,512]{1,0:T(8,128)S(1)} %get-tuple-element.87) | copy-start | bytes 73732
  184.3 12.0 %copy-start.12 = (bf16[1024,768]{0,1:T(8,128)(2,1)}, bf16[1024,768]{0,1:T(8,128)(2,1)S(1)}, u32[]{:S(2)}) copy-start(bf16[1024,768]{0,1:T(8,128)(2,1)S(1)} %convolution_convert_fusion.3) | copy-start | bytes 4718596
  184.3 12.0 %copy-start.21 = (bf16[1024,768]{0,1:T(8,128)(2,1)S(1)}, bf16[1024,768]{0,1:T(8,128)(2,1)}, u32[]{:S(2)}) copy-start(bf16[1024,768]{0,1:T(8,128)(2,1)} %convolution_convert_fusion.2) | copy-start | bytes 4718596
  212.1 11.0 %copy-start.13 = (bf16[1024,768]{0,1:T(8,128)(2,1)S(1)}, bf16[1024,768]{0,1:T(8,128)(2,1)}, u32[]{:S(2)}) copy-start(bf16[1024,768]{0,1:T(8,128)(2,1)} %copy-done.12) | copy-start | bytes 4718596
  223.1 10.5 copy-start.33
  235.0 52.8 %slice-start.5 = ((s8[4718592]{0:T(1024)(128)(4,1)}), s8[4194304]{0:T(1024)(128)(4,1)S(1)}, s32[]{:S(2)}) async-start(s8[4718592]{0:T(1024)(128)(4,1)} %bitcast.211), calls=%async_computation.30 | async-start | bytes 8388608
  239.7 48.2 %slice-start.6 = ((s8[4718592]{0:T(1024)(128)(4,1)}), s8[524288]{0:T(1024)(128)(4,1)S(1)}, s32[]{:S(2)}) async-start(s8[4718592]{0:T(1024)(128)(4,1)} %bitcast.211), calls=%async_computation.31 | async-start | bytes 1048576
  239.7 54.6 %slice-start.3 = ((s8[4718592]{0:T(1024)(128)(4,1)}), s8[4194304]{0:T(1024)(128)(4,1)S(1)}, s32[]{:S(2)}) async-start(s8[4718592]{0:T(1024)(128)(4,1)} %bitcast.209), calls=%async_computation.28 | async-start | bytes 8388608
  294.3 9.6 copy-start.54
  337.2 57.9 %all-to-all-start.1 = ((bf16[4,2,122880]{2,1,0:T(2,128)(2,1)}), bf16[4,2,122880]{2,1,0:T(2,128)(2,1)}, u32[]{:S(2)}, u32[]{:S(2)}) async-start(bf16[4,2,122880]{2,1,0:T(2,128)(2,1)} %reshape.390), calls=%async_computation.1 | async-start | bytes 3932160 | tf_op jit(solution)/shard_map/all_to_all | solution.py:179
  341.6 437.1 %reduce-scatter.20.cloned.1.call-start = ((), (), s32[]{:S(2)}) async-start(), calls=%async_computation.21 | async-start | bytes 10616832 | tf_op jit(solution)/shard_map/reduce_scatter | solution.py:323
  402.5 52.5 %slice-start.7 = ((s8[15728640]{0:T(1024)(128)(4,1)}), s8[4194304]{0:T(1024)(128)(4,1)S(1)}, s32[]{:S(2)}) async-start(s8[15728640]{0:T(1024)(128)(4,1)} %bitcast.213), calls=%async_computation.32 | async-start | bytes 8388608
  402.5 52.5 %slice-start.8 = ((s8[15728640]{0:T(1024)(128)(4,1)}), s8[4194304]{0:T(1024)(128)(4,1)S(1)}, s32[]{:S(2)}) async-start(s8[15728640]{0:T(1024)(128)(4,1)} %bitcast.213), calls=%async_computation.33 | async-start | bytes 8388608
  406.6 48.4 %slice-start.9 = ((s8[15728640]{0:T(1024)(128)(4,1)}), s8[4194304]{0:T(1024)(128)(4,1)S(1)}, s32[]{:S(2)}) async-start(s8[15728640]{0:T(1024)(128)(4,1)} %bitcast.213), calls=%async_computation.34 | async-start | bytes 8388608
  406.6 48.4 %slice-start.10 = ((s8[15728640]{0:T(1024)(128)(4,1)}), s8[3145728]{0:T(1024)(128)(4,1)S(1)}, s32[]{:S(2)}) async-start(s8[15728640]{0:T(1024)(128)(4,1)} %bitcast.213), calls=%async_computation.35 | async-start | bytes 6291456
  465.1 314.2 %reduce-scatter.18.cloned.1.call-start = ((), (), s32[]{:S(2)}) async-start(), calls=%async_computation.19 | async-start | bytes 10616832 | tf_op jit(solution)/shard_map/reduce_scatter | solution.py:322
  465.1 22.2 %copy-start.25 = (bf16[4,320,768]{2,1,0:T(8,128)(2,1)S(1)}, bf16[4,320,768]{2,1,0:T(8,128)(2,1)}, u32[]{:S(2)}) copy-start(bf16[4,320,768]{2,1,0:T(8,128)(2,1)} %copy-done.24) | copy-start | bytes 5898244
  539.5 47.9 %all-to-all-start.3 = ((bf16[4,2,122880]{2,1,0:T(2,128)(2,1)}), bf16[4,2,122880]{2,1,0:T(2,128)(2,1)}, u32[]{:S(2)}, u32[]{:S(2)}) async-start(bf16[4,2,122880]{2,1,0:T(2,128)(2,1)} %reshape.392), calls=%async_computation.3 | async-start | bytes 3932160 | tf_op jit(solution)/shard_map/all_to_all | solution.py:215
  543.9 237.4 %reduce-scatter.22.cloned.1.call-start = ((), (), s32[]{:S(2)}) async-start(), calls=%async_computation.23 | async-start | bytes 491520
  547.6 349.8 %reduce-scatter.16.cloned.1.call-start = ((), (), s32[]{:S(2)}) async-start(), calls=%async_computation.18 | async-start | bytes 2949120 | tf_op jit(solution)/shard_map/reduce_scatter | solution.py:302
  607.3 290.1 %reduce-scatter.14.cloned.1.call-start = ((), (), s32[]{:S(2)}) async-start(), calls=%async_computation.17 | async-start | bytes 2949120 | tf_op jit(solution)/shard_map/reduce_scatter | solution.py:301
  610.6 11.2 %copy-start.20 = (bf16[1024,768]{0,1:T(8,128)(2,1)}, bf16[1024,768]{0,1:T(8,128)(2,1)S(1)}, u32[]{:S(2)}) copy-start(bf16[1024,768]{0,1:T(8,128)(2,1)S(1)} %convolution_convert_fusion) | copy-start | bytes 4718596
  621.8 11.9 %copy-start.8 = (bf16[1024,768]{0,1:T(8,128)(2,1)S(1)}, bf16[1024,768]{0,1:T(8,128)(2,1)}, u32[]{:S(2)}) copy-start(bf16[1024,768]{0,1:T(8,128)(2,1)} %copy-done.6) | copy-start | bytes 4718596
  621.8 11.9 %copy-start.42 = (f32[768]{0:T(1024)S(1)}, f32[768]{0:T(1024)}, u32[]{:S(2)}) copy-start(f32[768]{0:T(1024)} %copy-done.41) | copy-start | bytes 9220
  621.8 11.9 %copy-start.44 = (f32[1024]{0:T(1024)S(1)}, f32[1024]{0:T(1024)}, u32[]{:S(2)}) copy-start(f32[1024]{0:T(1024)} %copy-done.43) | copy-start | bytes 12292
  668.7 228.7 %reduce-scatter.10.cloned.1.call-start = ((), (), s32[]{:S(2)}) async-start(), calls=%async_computation.15 | async-start | bytes 2949120 | tf_op jit(solution)/shard_map/reduce_scatter | solution.py:299
  668.8 26.1 %copy-start.5 = (bf16[1024,768]{0,1:T(8,128)(2,1)S(1)}, bf16[1024,768]{0,1:T(8,128)(2,1)}, u32[]{:S(2)}) copy-start(bf16[1024,768]{0,1:T(8,128)(2,1)} %copy-done.4) | copy-start | bytes 4718596
  752.9 144.5 %reduce-scatter.12.cloned.1.call-start = ((), (), s32[]{:S(2)}) async-start(), calls=%async_computation.16 | async-start | bytes 2949120 | tf_op jit(solution)/shard_map/reduce_scatter | solution.py:300
  778.6 199.8 %all-gather.18.cloned.1.call-start = ((), (), s32[]{:S(2)}) async-start(), calls=%async_computation.22 | async-start | bytes 10616832 | tf_op jit(solution)/shard_map/all_gather | solution.py:327
  779.2 199.3 %all-gather.16.cloned.1.call-start = ((), (), s32[]{:S(2)}) async-start(), calls=%async_computation.20 | async-start | bytes 10616832 | tf_op jit(solution)/shard_map/all_gather | solution.py:326
  780.0 258.5 %all-reduce.11.cloned.1.call-start = ((), (), s32[]{:S(2)}) async-start(), calls=%async_computation.24 | async-start | bytes 4718592 | tf_op jit(solution)/shard_map/psum | solution.py:308
  813.3 31.0 %copy-start.17 = (bf16[1024,768]{0,1:T(8,128)(2,1)S(1)}, bf16[1024,768]{0,1:T(8,128)(2,1)}, u32[]{:S(2)}) copy-start(bf16[1024,768]{0,1:T(8,128)(2,1)} %get-tuple-element.80) | copy-start | bytes 4718596
  898.9 39.7 %copy-start.48 = (f32[768]{0:T(1024)S(1)}, f32[768]{0:T(1024)}, u32[]{:S(2)}) copy-start(f32[768]{0:T(1024)} %get-tuple-element.60) | copy-start | bytes 9220
  1044.3 10.0 slice-start
  1045.1 9.2 slice-start.1
  1045.1 9.2 slice-start.2
  (35 other events, 106.6 us)
Sparse Core Ops, SparseCore 0:
  9.6 33.5 all-gather.9
  44.8 29.4 all-gather.11
  75.9 29.5 all-gather.7
  106.9 29.5 all-gather.13
  465.2 75.7 reduce-scatter.19
  544.9 76.4 reduce-scatter.17
  624.2 20.5 reduce-scatter.21
  647.3 46.2 reduce-scatter.15
  696.0 47.5 reduce-scatter.13
  753.0 47.1 reduce-scatter.9
  802.6 47.5 reduce-scatter.11
  852.1 58.3 all-gather.17
  912.6 58.7 all-gather.15
  975.1 63.3 all-reduce.10

commit v2 on v0

v2 whole, which is shorter than its diff:
```python
from functools import partial
import jax, jax.numpy as jnp
from jax import lax
from jax.experimental import pallas as pl
from jax.experimental.pallas import tpu as pltpu
from jax.sharding import PartitionSpec as P

f32, bf16 = jnp.float32, jnp.bfloat16
NN = (((1,), (0,)), ((), ()))
NT = (((1,), (1,)), ((), ()))
TN = (((0,), (0,)), ((), ()))
ROOT = 0.7978845608028654
CUBE = 0.044715


def dot(a, b, dims=NN):
    return lax.dot_general(a, b, dims, preferred_element_type=f32)


def attend_kernel(q_ref, k_ref, v_ref, aug_q_ref, aug_k_ref, line_ref, e_ref, att_ref, inv_ref, s_ref, k_nat, rows=256, cols=256):
    length = k_ref.shape[-1]
    band = 128
    k_nat[...] = jnp.concatenate([k_ref[0], aug_k_ref[...]], axis=0).T
    q_aug = jnp.concatenate([q_ref[0], aug_q_ref[0]], axis=0)
    v_aug = jnp.concatenate([v_ref[0], jnp.ones((16, length), bf16)], axis=0)
    line = jnp.broadcast_to(line_ref[0, 0:1, :], (band, 4 * band))
    skew = pltpu.roll(line, 0, 1, stride=1, stride_axis=0)
    near = [skew[:, (2 - o) * band : (3 - o) * band] for o in (-1, 0, 1)]
    width = v_ref.shape[1]
    for c in range(0, length, cols):
        top = None
        for r in range(0, length, rows):
            s = dot(k_nat[r : r + rows, :], q_aug[:, c : c + cols])
            pieces = []
            for i in range(r // band, (r + rows) // band):
                blocks = []
                for j in range(c // band, (c + cols) // band):
                    blk = s[i * band - r : (i + 1) * band - r, j * band - c : (j + 1) * band - c]
                    if abs(i - j) <= 1:
                        blk = blk + near[i - j + 1]
                    blocks.append(blk)
                pieces.append(jnp.concatenate(blocks, axis=1))
            s = jnp.concatenate(pieces, axis=0)
            s_ref[r : r + rows, :] = s
            m = jnp.max(s.reshape(rows // 8, 8, cols), axis=0)
            top = m if top is None else jnp.maximum(top, m)
        top = jnp.max(top, axis=0, keepdims=True)
        out = None
        for r in range(0, length, rows):
            e = jnp.exp(s_ref[r : r + rows, :] - top).astype(bf16)
            e_ref[0, r : r + rows, c : c + cols] = e
            part = dot(v_aug[:, r : r + rows], e)
            out = part if out is None else out + part
        inv = 1.0 / out[width : width + 1, :]
        inv_ref[0, :, c : c + cols] = jnp.broadcast_to(inv, (8, cols))
        att_ref[0, :, c : c + cols] = (out[:width] * inv).astype(bf16)


def attend(qkv, aug_q, aug_k, line, heads):
    width, length = qkv.shape[1:]
    head = lambda off: pl.BlockSpec((1, width, length), lambda h: (h + off, 0, 0))
    return pl.pallas_call(
        attend_kernel,
        grid=(heads,),
        in_specs=[head(0), head(heads), head(2 * heads),
                  pl.BlockSpec((1, 16, length), lambda h: (h, 0, 0)),
                  pl.BlockSpec((16, length), lambda h: (0, 0)),
                  pl.BlockSpec((1, 8, 512), lambda h: (h, 0, 0))],
        out_specs=[pl.BlockSpec((1, length, length), lambda h: (h, 0, 0)),
                   pl.BlockSpec((1, width, length), lambda h: (h, 0, 0)),
                   pl.BlockSpec((1, 8, length), lambda h: (h, 0, 0))],
        out_shape=[jax.ShapeDtypeStruct((heads, length, length), bf16),
                   jax.ShapeDtypeStruct((heads, width, length), bf16),
                   jax.ShapeDtypeStruct((heads, 8, length), f32)],
        scratch_shapes=[pltpu.VMEM((length, 256), f32), pltpu.VMEM((length, width + 16), bf16)],
        compiler_params=pltpu.CompilerParams(vmem_limit_bytes=40 * 2**20),
        cost_estimate=pl.CostEstimate(flops=heads * length * length * 256 * 4, bytes_accessed=heads * length * length * 2, transcendentals=heads * length * length),
        name="attend",
    )(qkv, qkv, qkv, aug_q, aug_k, line)


def pull_kernel(e_ref, g_ref, att_ref, inv_ref, q_ref, k_ref, v_ref, grad_ref, diag_ref, far_ref, v_nat, gs_ref, near_ref, rows=256, cols=256):
    length = k_ref.shape[-1]
    band = 128
    g = (g_ref[0].astype(f32) * inv_ref[0, 0:1, :]).astype(bf16)
    delta = jnp.sum(g.astype(f32) * att_ref[0].astype(f32), axis=0, keepdims=True)
    hi = delta.astype(bf16)
    lo = (delta - hi.astype(f32)).astype(bf16)
    pad = jnp.concatenate([hi.astype(f32), lo.astype(f32), jnp.zeros((14, length), f32)], axis=0)
    g_aug = jnp.concatenate([g, (-pad).astype(bf16)], axis=0)
    v_nat[...] = jnp.concatenate([v_ref[0], jnp.ones((16, length), bf16)], axis=0).T
    near_ref[...] = jnp.zeros_like(near_ref)
    far = [jnp.zeros((8, band), f32), jnp.zeros((8, band), f32)]
    for c in range(0, length, cols):
        for r in range(0, length, rows):
            gp = dot(v_nat[r : r + rows, :], g_aug[:, c : c + cols])
            gs = e_ref[0, r : r + rows, c : c + cols].astype(f32) * gp
            gs_ref[r : r + rows, c : c + cols] = gs.astype(bf16)
            for i in range(r // band, (r + rows) // band):
                for j in range(c // band, (c + cols) // band):
                    blk = gs[i * band - r : (i + 1) * band - r, j * band - c : (j + 1) * band - c]
                    if abs(i - j) <= 1:
                        lane = (2 - (i - j)) * band
                        near_ref[:, lane : lane + band] += blk
                    else:
                        side = int(i > j)
                        far[side] = far[side] + jnp.sum(blk.reshape(band // 8, 8, band), axis=0)
    skew = near_ref[0:8, :]
    for a in range(8, band, 8):
        skew = skew + pltpu.roll(near_ref[a : a + 8, :], 4 * band - a, 1)
    diag_ref[0] = skew
    far_ref[0] = jnp.concatenate(far, axis=1)
    grad_ref[2, 0] = dot(g, e_ref[0], NT).astype(bf16)
    grad_ref[1, 0] = dot(q_ref[0], gs_ref[...], NT).astype(bf16)
    grad_ref[0, 0] = dot(k_ref[0], gs_ref[...]).astype(bf16)


def pull(e, g, att, inv, qkv, heads):
    width, length = qkv.shape[1:]
    head = lambda off: pl.BlockSpec((1, width, length), lambda h: (h + off, 0, 0))
    return pl.pallas_call(
        pull_kernel,
        grid=(heads,),
        in_specs=[pl.BlockSpec((1, length, length), lambda h: (h, 0, 0)), head(0), head(0),
                  pl.BlockSpec((1, 8, length), lambda h: (h, 0, 0)), head(0), head(heads), head(2 * heads)],
        out_specs=[pl.BlockSpec((3, 1, width, length), lambda h: (0, h, 0, 0)),
                   pl.BlockSpec((1, 8, 512), lambda h: (h, 0, 0)),
                   pl.BlockSpec((1, 8, 256), lambda h: (h, 0, 0))],
        out_shape=[jax.ShapeDtypeStruct((3, heads, width, length), bf16), jax.ShapeDtypeStruct((heads, 8, 512), f32), jax.ShapeDtypeStruct((heads, 8, 256), f32)],
        scratch_shapes=[pltpu.VMEM((length, width + 16), bf16), pltpu.VMEM((length, length), bf16), pltpu.VMEM((128, 512), f32)],
        compiler_params=pltpu.CompilerParams(vmem_limit_bytes=40 * 2**20),
        cost_estimate=pl.CostEstimate(flops=heads * length * length * 256 * 8, bytes_accessed=heads * length * length * 2, transcendentals=0),
        name="pull",
    )(e, g, att, inv, qkv, qkv, qkv)


def bucket_of(r):
    n = jnp.abs(r)
    far = sum((n >= t).astype(jnp.int32) for t in (12, 16, 23, 32, 46, 64, 91))
    return jnp.where(n < 8, n, 8 + far) + 16 * (r > 0)


def helpers(segments, rel_bias):
    length = segments.shape[0]
    heads = rel_bias.shape[1]
    seg = (segments[None, :] == jnp.arange(4)[:, None]).astype(f32)
    blk = jnp.arange(length) // 128
    nb = length // 128
    own = (blk[None, :] == jnp.arange(nb)[:, None]).astype(f32)
    aug_k = jnp.concatenate([seg, own, jnp.zeros((12 - nb, length), f32)], 0).astype(bf16)
    left, right = rel_bias[15], rel_bias[31]
    kb = jnp.arange(nb)[:, None]
    c = jnp.where(kb < blk[None] - 1, left[:, None, None], jnp.where(kb > blk[None] + 1, right[:, None, None], 0))
    aug_q = jnp.concatenate([jnp.broadcast_to(-1e30 * (1 - seg), (heads, 4, length)), c.astype(f32), jnp.zeros((heads, 12 - nb, length), f32)], 1).astype(bf16)
    y = jnp.arange(512)
    hot = (bucket_of(-(y - 256))[None] == jnp.arange(rel_bias.shape[0])[:, None])
    line = jnp.einsum("bh,by->hy", rel_bias, hot.astype(bf16), preferred_element_type=f32)
    return aug_q, aug_k, jnp.broadcast_to(line[:, None], (heads, 8, 512))


def table_grad(diag, far, buckets):
    place = jnp.arange(512)[None, :] - jnp.arange(8)[:, None]
    hot = bucket_of(256 - place)[None] == jnp.arange(buckets)[:, None, None]
    t = jnp.einsum("kby,hby->kh", hot.astype(f32), diag, precision=lax.Precision.HIGHEST)
    l = jnp.sum(far[:, :, :128], (1, 2)); r = jnp.sum(far[:, :, 128:], (1, 2))
    b = jnp.arange(buckets)[:, None]
    return t + jnp.where(b == 15, l, 0) + jnp.where(b == 31, r, 0)


def expert_kernel(x_ref, g_ref, first_ref, second_ref, router_ref, mine_ref, *rest, experts):
    hid_ref, pre_ref, xs_ref, gs_ref, back_ref, log_ref, acc_ref, prob_ref, dot_ref = rest[-9:]
    step, last = pl.program_id(0), pl.num_programs(0) - 1
    x, g = x_ref[...], g_ref[...]

    @pl.when(step == 0)
    def _():
        lane = lax.broadcasted_iota(jnp.int32, prob_ref.shape, 1)
        logits = jnp.where(lane < experts, dot(x, router_ref[...]), -1e30)
        shifted = jnp.exp(logits - jnp.max(logits, axis=1, keepdims=True))
        prob_ref[...] = shifted / jnp.sum(shifted, axis=1, keepdims=True)
        acc_ref[...] = jnp.zeros_like(acc_ref)
        dot_ref[...] = jnp.zeros_like(dot_ref)

    gate = jnp.sum(prob_ref[...] * mine_ref[0:1, :], axis=1, keepdims=True)
    u = dot(x, first_ref[0])
    raw = dot(g, second_ref[0], NT)
    square = u * u
    t = jnp.tanh(u * (ROOT + (ROOT * CUBE) * square))
    half = 0.5 + 0.5 * t
    hidden = (u * half).astype(bf16)
    slope = half + (0.5 * u) * (1.0 - t * t) * (ROOT + (3.0 * ROOT * CUBE) * square)
    grad = (raw * gate * slope).astype(bf16)
    hid_ref[0] = hidden
    pre_ref[0] = grad
    paired = hidden.astype(f32) * raw
    total = dot_ref[...]
    for c in range(0, paired.shape[1], 128):
        total = total + paired[:, c : c + 128]
    dot_ref[...] = total
    acc_ref[...] += dot(grad, first_ref[0], NT)

    @pl.when(step == last)
    def _():
        probs = prob_ref[...]
        pull = jnp.sum(dot_ref[...], axis=1, keepdims=True)
        coming = mine_ref[0:1, :] * pull
        grad_logits = probs * (coming - jnp.sum(probs * coming, axis=1, keepdims=True))
        log_ref[...] = grad_logits
        high = grad_logits.astype(bf16)
        low = (grad_logits - high.astype(f32)).astype(bf16)
        more = dot(high, router_ref[...], NT) + dot(low, router_ref[...], NT)
        back_ref[...] = (acc_ref[...] + more).astype(bf16)
        xs_ref[0] = x
        gs_ref[0] = (g.astype(f32) * gate).astype(bf16)


def expert_pass(turn, turns, x, g, first, second, router, mine, kept, experts):
    rows, width = x.shape
    hidden = first.shape[2]
    cut = 512 if hidden % 512 == 0 else hidden
    whole = lambda *shape: pl.BlockSpec(shape, lambda s: (0,) * len(shape))
    hold = pl.BlockSpec((1, rows, cut), lambda s: (turn, 0, s))
    row = pl.BlockSpec((1, rows, width), lambda s: (turn, 0, 0))
    struct = jax.ShapeDtypeStruct
    return pl.pallas_call(
        partial(expert_kernel, experts=experts),
        grid=(hidden // cut,),
        in_specs=[
            whole(rows, width),
            whole(rows, width),
            pl.BlockSpec((1, width, cut), lambda s: (0, 0, s)),
            pl.BlockSpec((1, cut, width), lambda s: (0, s, 0)),
            whole(width, 128),
            whole(8, 128),
        ]
        + [pl.BlockSpec(memory_space=pl.ANY)] * len(kept),
        out_specs=[hold, hold, row, row, whole(rows, width), whole(rows, 128)],
        out_shape=[
            struct((turns, rows, hidden), bf16),
            struct((turns, rows, hidden), bf16),
            struct((turns, rows, width), bf16),
            struct((turns, rows, width), bf16),
            struct((rows, width), bf16),
            struct((rows, 128), f32),
        ],
        scratch_shapes=[
            pltpu.VMEM((rows, width), f32),
            pltpu.VMEM((rows, 128), f32),
            pltpu.VMEM((rows, 128), f32),
        ],
        input_output_aliases={6 + i: i for i in range(len(kept))},
        compiler_params=pltpu.CompilerParams(vmem_limit_bytes=40 * 2**20),
        cost_estimate=pl.CostEstimate(
            flops=6 * rows * width * hidden,
            bytes_accessed=4 * width * hidden + 4 * rows * hidden,
            transcendentals=rows * hidden,
        ),
        name="expert_pass",
    )(x, g, first, second, router, mine, *kept)


def rms_norm(values_in, gain_vec):
    return (
        values_in
        * lax.rsqrt(jnp.mean(values_in * values_in, axis=-1, keepdims=True) + 1e-06)
        * gain_vec
    )


def log2(n):
    return n.bit_length() - 1


def swap(x, axis, bit):
    n = lax.axis_size(axis)
    return lax.ppermute(x, axis, [(i, i ^ (1 << bit)) for i in range(n)])


def shift(x, axis, k):
    n = lax.axis_size(axis)
    return lax.ppermute(x, axis, [(i, (i + k) % n) for i in range(n)])


def side(axis, bit):
    return (lax.axis_index(axis) >> bit) & 1


def gather_bits(x, axis, dim, order):
    bits = log2(lax.axis_size(axis))
    for bit in order:
        other = swap(x, axis, bit)
        mine = side(axis, bit) == 1
        at = dim + bits - 1 - bit
        x = jnp.concatenate([jnp.where(mine, other, x), jnp.where(mine, x, other)], axis=at)
    return x


def reduce_bits(x, axis, dim, order):
    bits = log2(lax.axis_size(axis))
    for bit in order:
        at = dim + bits - 1 - bit
        mine = side(axis, bit)
        keep = lax.dynamic_index_in_dim(x, mine, at)
        away = lax.dynamic_index_in_dim(x, 1 - mine, at)
        x = (keep.astype(f32) + swap(away, axis, bit).astype(f32)).astype(bf16)
    return x


def paths(axis):
    bits = log2(lax.axis_size(axis))
    rest = list(range(1, bits))
    return rest, rest[::-1]


def spread(x, axis, ring, order):
    n, bits, m = lax.axis_size(axis), log2(lax.axis_size(axis)), lax.axis_size(ring)
    rows = x.shape[0] // n
    piece = lax.dynamic_slice_in_dim(x, lax.axis_index(axis) * rows, rows, 0)
    around = [piece] + [shift(piece, ring, m - k) for k in range(1, m)]
    double = jnp.stack(around + around)
    start = lax.rem(m - lax.axis_index(ring), m)
    held = lax.dynamic_slice_in_dim(double, start, m, 0)
    held = held.reshape((m,) + (1,) * bits + held.shape[1:])
    held = gather_bits(held, axis, 1, order + [0])
    return held.reshape(m * x.shape[0], x.shape[1])


def collect(x, axis, ring, order):
    n, bits, m = lax.axis_size(axis), log2(lax.axis_size(axis)), lax.axis_size(ring)
    rows, columns = x.shape
    x = x.reshape((m,) + (2,) * bits + (rows // m // n, columns))
    x = reduce_bits(x, axis, 1, [0] + order)
    me = lax.axis_index(ring)
    total = lax.dynamic_index_in_dim(x, me, 0).astype(f32)
    for k in range(1, m):
        away = lax.dynamic_index_in_dim(x, lax.rem(me + k, m), 0)
        total = total + shift(away, ring, k).astype(f32)
    x = gather_bits(total.astype(bf16), axis, 1, order[::-1] + [0])
    return x.reshape(rows // m, columns)


def total_of(x, axis):
    part = lax.psum_scatter(x, axis, scatter_dimension=0, tiled=True)
    return lax.all_gather(part, axis, axis=0, tiled=True)


def on_device(
    tokens,
    cotangent,
    segments,
    routes,
    w_query,
    w_key,
    w_value,
    w_output,
    norm_attn,
    norm_ffn,
    w_router,
    rel_bias,
    expert_input_weight,
    expert_output_weight,
):
    R, S = "replica", "shard"
    one, two = paths(R)
    rows, width = tokens.shape
    heads = rel_bias.shape[1]
    head = width // heads
    experts = w_router.shape[1]
    owned = w_query.shape[0]
    near = rel_bias.shape[0]
    me = lax.axis_index(S)
    capacity = 5 * rows // (4 * experts)

    extra = jnp.zeros((owned, 128), bf16)
    extra = extra.at[:, 0].set(norm_attn).at[:, 1].set(norm_ffn)
    extra = extra.at[:, 2 : 2 + experts].set(w_router).at[0 : rel_bias.shape[0], 8 : 8 + heads].set(rel_bias)
    cut = 3 * width // 2
    packed = jnp.concatenate([w_query, w_key, w_value], axis=1)
    part_one = spread(jnp.concatenate([packed[:, :cut], extra], 1), R, S, one)
    part_two = spread(packed[:, cut:], R, S, two)
    full_qkv = jnp.concatenate([part_one[:, :cut], part_two], axis=1)
    small = part_one[:, cut:]
    full_output = spread(w_output, R, S, one)
    gain_one = small[:, 0].astype(f32)
    gain_two = small[:, 1].astype(f32)
    router = small[:, 2 : 2 + experts]
    table = small.reshape(-1, owned, 128)[:, : rel_bias.shape[0], 8 : 8 + heads].reshape(-1, heads)
    buckets = table.shape[0]

    names = lax.rem(me + jnp.arange(experts, dtype=jnp.int32), experts)
    chosen = (names[:, None] == routes[:, 0][None, :]).astype(bf16)
    ids = jnp.arange(rows, dtype=jnp.int32)
    earlier = (ids[:, None] < ids[None, :]).astype(bf16)
    slot = jnp.dot(chosen, earlier, preferred_element_type=f32).astype(jnp.int32)
    places = (
        (chosen[:, None, :] == 1)
        & (slot[:, None, :] == jnp.arange(capacity, dtype=jnp.int32)[None, :, None])
    ).astype(bf16)

    def send(values):
        out = [dot(places[k], values).astype(bf16) for k in range(experts)]
        return [out[0]] + [shift(out[k], S, k) for k in range(1, experts)]

    def take(back):
        back = [back[0]] + [shift(back[k], S, experts - k) for k in range(1, experts)]
        return dot(places.reshape(-1, rows), jnp.concatenate(back, 0), TN)

    g_rows = send(cotangent)

    inputs = tokens.astype(f32)
    normed_one = rms_norm(inputs, gain_one).astype(bf16)
    qkv = lax.dot_general(full_qkv, normed_one, (((0,), (1,)), ((), ())), preferred_element_type=f32)
    qkv = qkv.astype(bf16).reshape(3 * heads, head, rows)
    aug_q, aug_k, line = helpers(segments[0], table)
    e, att, inv = attend(qkv, aug_q, aug_k, line, heads)
    att_t = att.reshape(width, rows)
    middle = inputs + dot(att_t, full_output, TN)
    normed_two = rms_norm(middle, gain_two).astype(bf16)
    x_rows = send(normed_two)

    logits = jnp.dot(normed_two, router, preferred_element_type=f32)
    gate_probs = jax.nn.softmax(logits, axis=-1)
    named = (routes == jnp.arange(experts, dtype=jnp.int32)[None, :]).astype(f32)
    chosen_gate = jnp.sum(gate_probs * named, axis=-1)

    router_wide = jnp.pad(router, ((0, 0), (0, 128 - experts)))
    mine = jnp.broadcast_to((jnp.arange(128) == me).astype(f32)[None], (8, 128))
    kept, backs, logs = (), [], []
    for k in range(experts):
        *kept, back, log = expert_pass(
            k, experts, x_rows[k], g_rows[k], expert_input_weight, expert_output_weight,
            router_wide, mine, kept, experts,
        )
        backs.append(back)
        logs.append(log)
    hid, pre, xs, gs = kept
    grad_normed_two = take(backs)
    hid_flat, pre_flat = hid.reshape(-1, hid.shape[2]), pre.reshape(-1, pre.shape[2])
    xs_flat, gs_flat = xs.reshape(-1, width), gs.reshape(-1, width)
    grad_second = dot(hid_flat, gs_flat, TN).astype(bf16)
    grad_first = dot(xs_flat, pre_flat, TN).astype(bf16)
    results = [dot(hid[k], expert_output_weight[0]).astype(bf16) for k in range(experts)]
    combined = take(results)
    mixed = (middle + chosen_gate[:, None] * combined).astype(bf16)
    total_second = total_of(grad_second, R)
    total_first = total_of(grad_first, R)
    grad_router = dot(xs_flat, jnp.concatenate(logs, 0).astype(bf16), TN)[:, :experts]

    grad_final = cotangent.astype(f32)
    grad_mid_norm, grad_gain_two = jax.vjp(rms_norm, middle, gain_two)[1](grad_normed_two)
    grad_middle = grad_final + grad_mid_norm
    grad_branch = grad_middle.astype(bf16)
    grad_wout = dot(att_t, grad_branch).astype(bf16)
    grad_att = dot(full_output, grad_branch, NT).astype(bf16).reshape(heads, head, rows)
    grad_qkv, diag, far = pull(e, grad_att, att, inv, qkv, heads)
    grad_qkv = grad_qkv.reshape(3 * width, rows)
    grad_table = table_grad(diag, far, buckets)
    grad_wqkv = lax.dot_general(
        normed_one, grad_qkv, (((0,), (1,)), ((), ())), preferred_element_type=f32
    ).astype(bf16)
    grad_normed_one = lax.dot_general(
        grad_qkv, full_qkv, (((0,), (1,)), ((), ())), preferred_element_type=f32
    )
    grad_in_norm, grad_gain_one = jax.vjp(rms_norm, inputs, gain_one)[1](grad_normed_one)
    grad_inputs = grad_middle + grad_in_norm

    rest = jnp.zeros((width, 128), bf16)
    rest = rest.at[:, 0].set(grad_gain_one.astype(bf16)).at[:, 1].set(grad_gain_two.astype(bf16))
    rest = rest.at[:, 2 : 2 + experts].set(grad_router.astype(bf16))
    rest = rest.reshape(-1, owned, 128).at[:, :near, 8 : 8 + heads].set(
        grad_table.astype(bf16).reshape(-1, near, heads)
    ).reshape(width, 128)
    sum_out = collect(grad_wout, R, S, one).astype(f32)
    sum_one = collect(jnp.concatenate([grad_wqkv[:, :cut], rest], 1), R, S, one).astype(f32)
    sum_two = collect(grad_wqkv[:, cut:], R, S, two).astype(f32)
    sum_rest = sum_one[:, cut:]
    return (
        mixed,
        grad_inputs,
        sum_one[:, :width],
        jnp.concatenate([sum_one[:, width:cut], sum_two[:, : 2 * width - cut]], 1),
        sum_two[:, 2 * width - cut :],
        sum_out,
        sum_rest[:, 0],
        sum_rest[:, 1],
        sum_rest[:, 2 : 2 + experts],
        sum_rest[:near, 8 : 8 + heads],
        total_first.astype(f32)[None],
        total_second.astype(f32)[None],
    )


def solution(mesh):
    rows = P(("replica", "shard"), None)
    own, vec, cube = P("shard", None), P("shard"), P("shard", None, None)
    return jax.shard_map(
        on_device,
        mesh=mesh,
        in_specs=(rows,) * 4 + (own,) * 4 + (vec,) * 2 + (own,) * 2 + (cube,) * 2,
        out_specs=(rows,) * 2 + (own,) * 4 + (vec,) * 2 + (own,) * 2 + (cube,) * 2,
        check_vma=False,
    )
```

time: 1080 us -> 553 us (0.51)
  matrix products: 387 us -> 81.4 us
  blocking collectives: 203 us -> 0 us
  local copies, waits for them, and re-layouts: 227 us -> 49.1 us
  starting transfers between devices: 9.45 us -> 120 us
  Pallas kernels: 0 us -> 106 us
  other arithmetic: 121 us -> 53.2 us
  waiting for transfers between devices: 104 us -> 119 us
    dot_general x40 -> x27, matrix products: 383 us -> 81.4 us  [the longest x20 63.4 us: dot(): return lax.dot_general(a, b, dims, preferred_element_type=f32)]
    ppermute x0 -> x57, starting transfers between devices: none -> 120 us  [the longest x30 93.4 us: shift(): return lax.ppermute(x, axis, [(i, (i + k) % n) for i in range(n)])]
    ppermute x0 -> x57, waiting for transfers between devices: none -> 119 us  [the longest x27 65.6 us: swap(): return lax.ppermute(x, axis, [(i, i ^ 1 << bit) for i in range(n)])]
    pallas_call x0 -> x6, Pallas kernels: none -> 106 us  [the longest x4 43.8 us: expert_pass(): pl.pallas_call(partial(expert_kernel, experts=experts), grid=(hidden // c...]
    all_to_all x2 -> x0, blocking collectives: 88.8 us -> none  [the longest x1 44.4 us: on_device(): lax.all_to_all(outgoing, 'shard', split_axis=0, concat_axis=1, tiled=True)]
    mul x2 -> x0, local copies, waits for them, and re-layouts: 62 us -> none  [on_device(): grad_scores = chances * (grad_chances - inner_sum)]
    all_gather x2 -> x0, blocking collectives: 60.9 us -> none  [the longest x1 48.8 us: on_device(): lax.all_gather(w_router, 'shard', axis=0, tiled=True)]
    dot_general x2 -> x0, local copies, waits for them, and re-layouts: 60.5 us -> none  [block_scores(): jnp.einsum('rni,rf->fni', slot_indicators, relative_bias_table, preferred...]
  transfers between devices with their start and end apart: 16 -> 61, of which waited for: 2 -> 27; matrix products, arithmetic and copies ran while one was open for 58% -> 28% of each run, Pallas kernels for 0% -> 17%
where the time goes in v2:
time: 553 us; the launch traced here: 545 us
  starting transfers between devices  120 us (22%)
  waiting for transfers between devices  119 us (22%)
  Pallas kernels  106 us (19%)
  matrix products  81.4 us (15%)
  other arithmetic  53.2 us (10%)
  local copies, waits for them, and re-layouts  49.1 us (9%)
  between operations  15.8 us (3%)
    ppermute x30, starting transfers between devices, shift(): return lax.ppermute(x, axis, [(i, (i + k) % n) for i in range(n)])  93.4 us
    ppermute x27, waiting for transfers between devices, swap(): return lax.ppermute(x, axis, [(i, i ^ 1 << bit) for i in range(n)])  65.6 us
    dot_general x20, matrix products, dot(): return lax.dot_general(a, b, dims, preferred_element_type=f32)  63.4 us
    ppermute x30, waiting for transfers between devices, shift(): return lax.ppermute(x, axis, [(i, (i + k) % n) for i in range(n)])  53.8 us
    pallas_call x4, Pallas kernels, expert_pass(): pl.pallas_call(partial(expert_kernel, experts=experts), grid=(hidden // c...  43.8 us
    unnamed x151, local copies, waits for them, and re-layouts  34.3 us
    pallas_call x1, Pallas kernels, pull(): pl.pallas_call(pull_kernel, grid=(heads,), in_specs=[pl.BlockSpec((1, len...  31.7 us
    pallas_call x1, Pallas kernels, attend(): pl.pallas_call(attend_kernel, grid=(heads,), in_specs=[head(0), head(head...  30.2 us
  transfers between devices with their start and end apart: 61, of which 27 were waited for; matrix products, arithmetic and copies ran while one was open for 28% of the time, Pallas kernels for 17%

profile of v2, /device:TPU:0, one launch (start us, length us, event | category | flops | bytes accessed | tf_op | source)
XLA Modules:
  0.0 545.1 jit_solution(1361055430736779538)
XLA Ops:
  8.1 5.1 collective-permute-start.6
  15.7 2.8 collective-permute-start.12
  46.4 3.8 collective-permute-start
  59.4 3.3 collective-permute-start.19
  71.7 3.5 collective-permute-done.15
  79.4 4.2 collective-permute-done.3
  89.0 3.0 collective-permute-done.10
  92.2 4.0 collective-permute-done.4
  102.4 4.5 convolution_convert_fusion
  107.0 30.2 %attend.1 = (bf16[12,1024,1024]{2,1,0:T(8,128)(2,1)}, bf16[12,64,1024]{2,1,0:T(8,128)(2,1)S(1)}, f32[12,8,1024]{2,1,0:T(8,128)S(1)}) custom-call(bf16[36,64,1024]{2,1,0:T(8,128)(2,1)S(1)} %bitcast.186, bf16[36,64,1024]{2,1,0:T(8,128)(2,1)S(1)} %bitcast.187, bf16[36,64,1024]{2,1,0:T(8,128)(2,1)S(1)} %bitcast.188, ...), custom_call_target="tpu_custom_call" | custom-call | flops 12884901888 | bytes 25165824 | tf_op jit(solution)/shard_map/attend/pallas_call | solution.py:62
  144.1 9.7 %collective-permute-start.20 = (bf16[320,768]{1,0:T(8,128)(2,1)S(1)}, bf16[320,768]{1,0:T(8,128)(2,1)S(1)}, u32[]{:S(2)}, u32[]{:S(2)}) collective-permute-start(bf16[320,768]{1,0:T(8,128)(2,1)S(1)} %convolution_convert_fusion.9), channel_id=1, source_target_pairs={{0,2},{1,3},{2,0},{3,1},{4,6},{5,7},{6,4},{7,5},{8,10},{9,11},{10,... | collective-permute-start | bytes 1474568 | tf_op jit(solution)/shard_map/ppermute | solution.py:281
  154.4 10.9 %expert_pass.4 = (bf16[4,320,3072]{2,1,0:T(8,128)(2,1)}, bf16[4,320,3072]{2,1,0:T(8,128)(2,1)}, bf16[4,320,768]{2,1,0:T(8,128)(2,1)S(1)}, bf16[4,320,768]{2,1,0:...) custom-call(bf16[320,768]{1,0:T(8,128)(2,1)S(1)} %convolution_convert_fusion.5.x_ref, ...), custom_call_target="tpu_custom_call" | custom-call | flops 4529848320 | bytes 13369344 | tf_op jit(solution)/shard_map/expert_pass/pallas_call | solution.py:225
  166.0 3.8 collective-permute-start.18
  169.8 9.2 %collective-permute-done.22.x_ref = bf16[320,768]{1,0:T(8,128)(2,1)S(1)} collective-permute-done((bf16[320,768]{1,0:T(8,128)(2,1)S(1)}, bf16[320,768]{1,0:T(8,128)(2,1)S(1)}, u32[]{:S(2)}, u32[]{:S(2)}) %collective-permute-start.22) | collective-permute-done | bytes 491552 | tf_op jit(solution)/shard_map/ppermute | solution.py:281
  179.0 10.8 %expert_pass.5 = (bf16[4,320,3072]{2,1,0:T(8,128)(2,1)}, bf16[4,320,3072]{2,1,0:T(8,128)(2,1)}, bf16[4,320,768]{2,1,0:T(8,128)(2,1)S(1)}, bf16[4,320,768]{2,1,0:...) custom-call(bf16[320,768]{1,0:T(8,128)(2,1)S(1)} %collective-permute, ...), custom_call_target="tpu_custom_call", output_to_operand_aliasing={{0}: (6, {}), {1}: (7, {}), {2}: (8, {}), {3}: (9, {})} | custom-call | flops 4529848320 | bytes 13369344 | tf_op jit(solution)/shard_map/expert_pass/pallas_call | solution.py:225
  189.8 11.0 %expert_pass.6 = (bf16[4,320,3072]{2,1,0:T(8,128)(2,1)}, bf16[4,320,3072]{2,1,0:T(8,128)(2,1)}, bf16[4,320,768]{2,1,0:T(8,128)(2,1)S(1)}, bf16[4,320,768]{2,1,0:...) custom-call(bf16[320,768]{1,0:T(8,128)(2,1)S(1)} %collective-permute, ...), custom_call_target="tpu_custom_call", output_to_operand_aliasing={{0}: (6, {}), {1}: (7, {}), {2}: (8, {}), {3}: (9, {})} | custom-call | flops 4529848320 | bytes 13369344 | tf_op jit(solution)/shard_map/expert_pass/pallas_call | solution.py:225
  200.9 11.0 %expert_pass.7 = (bf16[4,320,3072]{2,1,0:T(8,128)(2,1)}, bf16[4,320,3072]{2,1,0:T(8,128)(2,1)}, bf16[4,320,768]{2,1,0:T(8,128)(2,1)S(1)}, bf16[4,320,768]{2,1,0:...) custom-call(bf16[320,768]{1,0:T(8,128)(2,1)S(1)} %collective-permute, ...), custom_call_target="tpu_custom_call", output_to_operand_aliasing={{0}: (6, {}), {1}: (7, {}), {2}: (8, {}), {3}: (9, {})} | custom-call | flops 4529848320 | bytes 13369344 | tf_op jit(solution)/shard_map/expert_pass/pallas_call | solution.py:225
  213.2 11.1 %bitcast_convert_fusion.1 = bf16[768,3072]{1,0:T(8,128)(2,1)} fusion(bf16[4,320,768]{2,1,0:T(8,128)(2,1)S(1)} %get-tuple-element.159, bf16[4,320,3072]{2,1,0:T(8,128)(2,1)} %get-tuple-element.166), kind=kOutput, calls=%fused_computation.1 | convolution fusion | flops 6042157056 | bytes 14548992 | tf_op jit(solution)/shard_map/dot_general | solution.py:17
  224.6 2.6 copy.55
  233.8 5.5 %fusion.61 = bf16[320,768]{1,0:T(8,128)(2,1)} fusion(bf16[1,3072,768]{2,1,0:T(8,128)(2,1)} %second_ref.7, bf16[4,320,3072]{2,1,0:T(8,128)(2,1)} %get-tuple-element.151), kind=kOutput, calls=%fused_computation.83 | convolution fusion | flops 1510195200 | bytes 7176192 | tf_op jit(solution)/shard_map/dot_general | solution.py:17
  239.4 18.6 %collective-permute-start.26 = (bf16[320,768]{1,0:T(8,128)(2,1)}, bf16[320,768]{1,0:T(8,128)(2,1)}, u32[]{:S(2)}, u32[]{:S(2)}) collective-permute-start(bf16[320,768]{1,0:T(8,128)(2,1)} %fusion.61), channel_id=1, source_target_pairs={{0,1},{1,2},{2,3},{3,0},{4,5},{5,6},{6,7},{7,4},{8,9},{9,10},{10,1... | collective-permute-start | bytes 1474568 | tf_op jit(solution)/shard_map/ppermute | solution.py:281
  258.0 5.4 fusion.56
  265.8 2.9 collective-permute-start.28
  271.9 8.2 %bitcast_convert_fusion = bf16[3072,768]{1,0:T(8,128)(2,1)} fusion(bf16[4,320,3072]{2,1,0:T(8,128)(2,1)S(1)} %bitcast.200, bf16[4,320,768]{2,1,0:T(8,128)(2,1)S(1)} %copy-done.1), kind=kOutput, calls=%fused_computation | convolution fusion | flops 6042157056 | bytes 14548992 | tf_op jit(solution)/shard_map/dot_general | solution.py:17
  282.1 5.6 %fusion.46 = bf16[320,768]{1,0:T(8,128)(2,1)} fusion(bf16[1,3072,768]{2,1,0:T(8,128)(2,1)} %second_ref.7, bf16[4,320,3072]{2,1,0:T(8,128)(2,1)} %get-tuple-element.151), kind=kOutput, calls=%fused_computation.80 | convolution fusion | flops 1510195200 | bytes 7176192 | tf_op jit(solution)/shard_map/dot_general | solution.py:17
  287.7 3.5 collective-permute-done.29
  291.4 29.5 %collective-permute-done.28 = bf16[320,768]{1,0:T(8,128)(2,1)} collective-permute-done((bf16[320,768]{1,0:T(8,128)(2,1)}, bf16[320,768]{1,0:T(8,128)(2,1)}, u32[]{:S(2)}, u32[]{:S(2)}) %collective-permute-start.28) | collective-permute-done | bytes 491552 | tf_op jit(solution)/shard_map/ppermute | solution.py:281
  321.0 4.6 multiply_reduce_fusion
  329.9 31.7 %pull.1 = (bf16[3,12,64,1024]{3,2,1,0:T(8,128)(2,1)S(1)}, f32[12,8,512]{2,1,0:T(8,128)S(1)}, f32[12,8,256]{2,1,0:T(8,128)S(1)}) custom-call(bf16[12,1024,1024]{2,1,0:T(8,128)(2,1)} %get-tuple-element.156.e_ref, bf16[12,64,1024]{2,1,0:T(8,128)(2,1)S(1)} %bitcast.198, bf16[12,64,1024]{2,1,0:T(8,128)(2,1)S(1)} %copy-done.4, ...), custom_call_target="tpu_custom_call" | custom-call | flops 25769803776 | bytes 25165824 | tf_op jit(solution)/shard_map/pull/pallas_call | solution.py:121
  361.7 4.2 convolution_convert_fusion.1
  368.9 5.8 %fusion.14 = (bf16[768]{0:T(1024)(128)(2,1)S(1)}, f32[1024]{0:T(1024)S(1)}, f32[1024,768]{0,1:T(8,128)}) fusion(bf16[1024,768]{0,1:T(8,128)(2,1)S(1)} %copy-done.8, f32[1024]{0:T(1024)S(1)} %copy-done.42, f32[768]{0:T(1024)S(1)} %copy-done.40, bf16[2304,1024]{1,0:T(8,128)(2,1)S(1)} %bitcast.195, bf16[768,1152]{1,0:T(8,128)(2,1)S(1)} %bitcast.217, ...), kind=kOutput, calls=%fused_computation.31 | convolution fusion | flops 3636459776 | bytes 12988928 | tf_op jit(solution)/shard_map/dot_general | solution.py:461
  378.8 5.8 %fusion.16 = f32[1024,768]{0,1:T(8,128)} fusion(f32[1024,768]{0,1:T(8,128)} %copy-done.11, bf16[1024,768]{0,1:T(8,128)(2,1)} %copy-done.7, f32[1024,768]{0,1:T(8,128)} %get-tuple-element.264, f32[1024]{0:T(1024)S(1)} %multiply_multiply_fusion, f32[768]{0:T(1024)S(1)} %copy-done.40, f32[1024]{0:T(1024)S(1)} %copy-done.42), kind=kLoop, calls=%fused_computation.33 | loop fusion | flops 5505024 | bytes 11021312 | tf_op jit(solution)/shard_map/add | solution.py:465
  387.2 6.4 %add_convert_fusion = bf16[1024,768]{0,1:T(8,128)(2,1)} fusion(f32[1024,768]{0,1:T(8,128)} %copy-done.9, f32[1024]{0:T(1024)S(1)} %fusion.105, pred[1280,1024]{1,0:T(32,128)(4,1)} %fusion.1, bf16[320,768]{1,0:T(8,128)(2,1)} %collective-permute-done.26, bf16[320,768]{1,0:T(8,128)(2,1)} %collective-permute-done.25, ...), kind=kOutput, calls=%fused_computation.38 | convolution fusion | flops 2023489536 | bytes 7999488 | tf_op jit(solution)/shard_map/dot_general | solution.py:17
  399.5 3.5 copy.64
  403.1 2.8 scatter.39
  409.6 5.1 collective-permute-done.50
  414.8 28.5 %collective-permute-start.53 = (bf16[1,1,1,1,24,768]{5,4,3,2,1,0:T(8,128)(2,1)S(1)}, bf16[1,1,1,1,24,768]{5,4,3,2,1,0:T(8,128)(2,1)S(1)}, u32[]{:S(2)}, u32[]{:S(2)}) collective-permute-start(bf16[1,1,1,1,24,768]{5,4,3,2,1,0:T(8,128)(2,1)S(1)} %get-tuple-element.247), channel_id=1, source_target_pairs={{0,3},{1,0},{2,1},{3,2},{4,7},{5,4},{6,5},{7,6},{8,11},{9,8},{10,9... | collective-permute-start | bytes 110600 | tf_op jit(solution)/shard_map/ppermute | solution.py:281
  445.3 2.8 collective-permute-done.52
  450.7 5.1 collective-permute-done.54
  458.1 3.1 collective-permute-done.55
  463.8 10.0 %collective-permute-done.41 = bf16[4,1,1,1,24,1152]{5,4,3,2,1,0:T(8,128)(2,1)S(1)} collective-permute-done((bf16[4,1,1,1,24,1152]{5,4,3,2,1,0:T(8,128)(2,1)S(1)}, bf16[4,1,1,1,24,1152]{5,4,3,2,1,0:T(8,128)(2,1)S(1)}, u32[]{:S(2)}, u32[]{:S(2)}) %collective-permute-start.41) | collective-permute-done | bytes 221216 | tf_op jit(solution)/shard_map/ppermute | solution.py:276
  473.9 3.2 collective-permute-start.44
  479.6 2.6 collective-permute-done.43
  487.9 9.2 %collective-permute-done.32 = bf16[4,1,1,1,24,1280]{5,4,3,2,1,0:T(8,128)(2,1)S(1)} collective-permute-done((bf16[4,1,1,1,24,1280]{5,4,3,2,1,0:T(8,128)(2,1)S(1)}, bf16[4,1,1,1,24,1280]{5,4,3,2,1,0:T(8,128)(2,1)S(1)}, u32[]{:S(2)}, u32[]{:S(2)}) %collective-permute-start.32) | collective-permute-done | bytes 245792 | tf_op jit(solution)/shard_map/ppermute | solution.py:276
  507.1 3.4 collective-permute-done.36
  510.8 7.4 %collective-permute-done.37 = bf16[1,2,1,1,24,1280]{5,4,3,2,1,0:T(8,128)(2,1)S(1)} collective-permute-done((bf16[1,2,1,1,24,1280]{5,4,3,2,1,0:T(8,128)(2,1)S(1)}, bf16[1,2,1,1,24,1280]{5,4,3,2,1,0:T(8,128)(2,1)S(1)}, u32[]{:S(2)}, u32[]{:S(2)}) %collective-permute-start.37) | collective-permute-done | bytes 122912 | tf_op jit(solution)/shard_map/ppermute | solution.py:276
  523.9 7.4 %bitcast_convert_fusion.3 = f32[1,768,3072]{2,1,0:T(8,128)} fusion(bf16[768,3072]{1,0:T(8,128)(2,1)} %all-gather.3.cloned.1.call-done), kind=kLoop, calls=%fused_computation.16 | loop fusion | flops 2359296 | bytes 14155776 | tf_op jit(solution)/shard_map/broadcast_in_dim | solution.py:488
  531.3 6.8 %bitcast_convert_fusion.2 = f32[1,3072,768]{2,1,0:T(8,128)} fusion(bf16[3072,768]{1,0:T(8,128)(2,1)} %all-gather.5.cloned.1.call-done), kind=kLoop, calls=%fused_computation.15 | loop fusion | flops 2359296 | bytes 14155776 | tf_op jit(solution)/shard_map/broadcast_in_dim | solution.py:489
  (424 shorter events, 146.1 us)
Async XLA Ops:
  7.2 370.4 %reduce-scatter.3.cloned.1.call-start = ((), (), s32[]{:S(2)}) async-start(), calls=%async_computation.2 | async-start | bytes 5308416 | tf_op jit(solution)/shard_map/reduce_scatter | solution.py:343
  8.1 49.8 %collective-permute-start.6 = (bf16[24,1152]{1,0:T(8,128)(2,1)S(1)}, bf16[24,1152]{1,0:T(8,128)(2,1)}, u32[]{:S(2)}, u32[]{:S(2)}) collective-permute-start(bf16[24,1152]{1,0:T(8,128)(2,1)S(1)} %get-tuple-element.207), channel_id=1, source_target_pairs={{0,3},{1,0},{2,1},{3,2},{4,7},{5,4},{6,5},{7,6},{8,11},{9,8},{10,9... | collective-permute-start | bytes 165896 | tf_op jit(solution)/shard_map/ppermute | solution.py:281
  13.2 46.2 %collective-permute-start.7 = (bf16[24,1152]{1,0:T(8,128)(2,1)S(1)}, bf16[24,1152]{1,0:T(8,128)(2,1)}, u32[]{:S(2)}, u32[]{:S(2)}) collective-permute-start(bf16[24,1152]{1,0:T(8,128)(2,1)S(1)} %get-tuple-element.207), channel_id=1, source_target_pairs={{0,2},{1,3},{2,0},{3,1},{4,6},{5,7},{6,4},{7,5},{8,10},{9,11},{10,... | collective-permute-start | bytes 165896 | tf_op jit(solution)/shard_map/ppermute | solution.py:281
  13.2 50.3 %collective-permute-start.8 = (bf16[24,1152]{1,0:T(8,128)(2,1)S(1)}, bf16[24,1152]{1,0:T(8,128)(2,1)}, u32[]{:S(2)}, u32[]{:S(2)}) collective-permute-start(bf16[24,1152]{1,0:T(8,128)(2,1)S(1)} %get-tuple-element.207), channel_id=1, source_target_pairs={{0,1},{1,2},{2,3},{3,0},{4,5},{5,6},{6,7},{7,4},{8,9},{9,10},{10,1... | collective-permute-start | bytes 165896 | tf_op jit(solution)/shard_map/ppermute | solution.py:281
  15.7 29.3 %collective-permute-start.12 = (bf16[24,768]{1,0:T(8,128)(2,1)}, bf16[24,768]{1,0:T(8,128)(2,1)}, u32[]{:S(2)}, u32[]{:S(2)}) collective-permute-start(bf16[24,768]{1,0:T(8,128)(2,1)} %get-tuple-element.203), channel_id=1, source_target_pairs={{0,3},{1,0},{2,1},{3,2},{4,7},{5,4},{6,5},{7,6},{8,11},{9,8},{10,9... | collective-permute-start | bytes 110600 | tf_op jit(solution)/shard_map/ppermute | solution.py:281
  18.5 27.9 %collective-permute-start.13 = (bf16[24,768]{1,0:T(8,128)(2,1)}, bf16[24,768]{1,0:T(8,128)(2,1)}, u32[]{:S(2)}, u32[]{:S(2)}) collective-permute-start(bf16[24,768]{1,0:T(8,128)(2,1)} %get-tuple-element.203), channel_id=1, source_target_pairs={{0,2},{1,3},{2,0},{3,1},{4,6},{5,7},{6,4},{7,5},{8,10},{9,11},{10,... | collective-permute-start | bytes 110600 | tf_op jit(solution)/shard_map/ppermute | solution.py:281
  45.0 6.6 %collective-permute-start.14 = (bf16[24,768]{1,0:T(8,128)(2,1)}, bf16[24,768]{1,0:T(8,128)(2,1)S(1)}, u32[]{:S(2)}, u32[]{:S(2)}) collective-permute-start(bf16[24,768]{1,0:T(8,128)(2,1)} %get-tuple-element.203), channel_id=1, source_target_pairs={{0,1},{1,2},{2,3},{3,0},{4,5},{5,6},{6,7},{7,4},{8,9},{9,10},{10,1... | collective-permute-start | bytes 110600 | tf_op jit(solution)/shard_map/ppermute | solution.py:281
  46.4 21.7 %collective-permute-start = (bf16[24,1280]{1,0:T(8,128)(2,1)S(1)}, bf16[24,1280]{1,0:T(8,128)(2,1)S(1)}, u32[]{:S(2)}, u32[]{:S(2)}) collective-permute-start(bf16[24,1280]{1,0:T(8,128)(2,1)S(1)} %get-tuple-element.205), channel_id=1, source_target_pairs={{0,3},{1,0},{2,1},{3,2},{4,7},{5,4},{6,5},{7,6},{8,11},{9,8},{10,9... | collective-permute-start | bytes 184328 | tf_op jit(solution)/shard_map/ppermute | solution.py:281
  51.6 16.8 %collective-permute-start.1 = (bf16[24,1280]{1,0:T(8,128)(2,1)S(1)}, bf16[24,1280]{1,0:T(8,128)(2,1)S(1)}, u32[]{:S(2)}, u32[]{:S(2)}) collective-permute-start(bf16[24,1280]{1,0:T(8,128)(2,1)S(1)} %get-tuple-element.205), channel_id=1, source_target_pairs={{0,2},{1,3},{2,0},{3,1},{4,6},{5,7},{6,4},{7,5},{8,10},{9,11},{10,... | collective-permute-start | bytes 184328 | tf_op jit(solution)/shard_map/ppermute | solution.py:281
  58.0 12.0 %collective-permute-start.2 = (bf16[24,1280]{1,0:T(8,128)(2,1)S(1)}, bf16[24,1280]{1,0:T(8,128)(2,1)S(1)}, u32[]{:S(2)}, u32[]{:S(2)}) collective-permute-start(bf16[24,1280]{1,0:T(8,128)(2,1)S(1)} %get-tuple-element.205), channel_id=1, source_target_pairs={{0,1},{1,2},{2,3},{3,0},{4,5},{5,6},{6,7},{7,4},{8,9},{9,10},{10,1... | collective-permute-start | bytes 184328 | tf_op jit(solution)/shard_map/ppermute | solution.py:281
  59.4 141.4 %collective-permute-start.19 = (bf16[320,768]{1,0:T(8,128)(2,1)}, bf16[320,768]{1,0:T(8,128)(2,1)S(1)}, u32[]{:S(2)}, u32[]{:S(2)}) collective-permute-start(bf16[320,768]{1,0:T(8,128)(2,1)} %convolution_convert_fusion.10), channel_id=1, source_target_pairs={{0,3},{1,0},{2,1},{3,2},{4,7},{5,4},{6,5},{7,6},{8,11},{9,8},{10,9... | collective-permute-start | bytes 1474568 | tf_op jit(solution)/shard_map/ppermute | solution.py:281
  63.6 126.2 %collective-permute-start.21 = (bf16[320,768]{1,0:T(8,128)(2,1)}, bf16[320,768]{1,0:T(8,128)(2,1)S(1)}, u32[]{:S(2)}, u32[]{:S(2)}) collective-permute-start(bf16[320,768]{1,0:T(8,128)(2,1)} %convolution_convert_fusion.8), channel_id=1, source_target_pairs={{0,2},{1,3},{2,0},{3,1},{4,6},{5,7},{6,4},{7,5},{8,10},{9,11},{10,... | collective-permute-start | bytes 1474568 | tf_op jit(solution)/shard_map/ppermute | solution.py:281
  68.1 97.9 %collective-permute-start.23 = (bf16[320,768]{1,0:T(8,128)(2,1)S(1)}, bf16[320,768]{1,0:T(8,128)(2,1)S(1)}, u32[]{:S(2)}, u32[]{:S(2)}) collective-permute-start(bf16[320,768]{1,0:T(8,128)(2,1)S(1)} %copy-done.51), channel_id=1, source_target_pairs={{0,1},{1,2},{2,3},{3,0},{4,5},{5,6},{6,7},{7,4},{8,9},{9,10},{10,1... | collective-permute-start | bytes 1474568 | tf_op jit(solution)/shard_map/ppermute | solution.py:281
  68.4 6.7 %collective-permute-start.15 = (bf16[4,1,1,1,24,768]{5,4,3,2,1,0:T(8,128)(2,1)S(1)}, bf16[4,1,1,1,24,768]{5,4,3,2,1,0:T(8,128)(2,1)S(1)}, u32[]{:S(2)}, u32[]{:S(2)}) collective-permute-start(bf16[4,1,1,1,24,768]{5,4,3,2,1,0:T(8,128)(2,1)S(1)} %dynamic-slice_bitcast_fusion.2), channel_id=1, source_target_pairs={{0,8},{4,12},{8,0},{12,4},{16,24},{20,28},{24,16},{28,20},{1,9},{5... | collective-permute-start | bytes 442376 | tf_op jit(solution)/shard_map/ppermute | solution.py:276
  70.0 7.9 %collective-permute-start.9 = (bf16[4,1,1,1,24,1152]{5,4,3,2,1,0:T(8,128)(2,1)S(1)}, bf16[4,1,1,1,24,1152]{5,4,3,2,1,0:T(8,128)(2,1)S(1)}, u32[]{:S(2)}, u32[]{:S(2)}) collective-permute-start(bf16[4,1,1,1,24,1152]{5,4,3,2,1,0:T(8,128)(2,1)S(1)} %dynamic-slice_bitcast_fusion.1), channel_id=1, source_target_pairs={{0,16},{4,20},{8,24},{12,28},{16,0},{20,4},{24,8},{28,12},{1,17},{... | collective-permute-start | bytes 663560 | tf_op jit(solution)/shard_map/ppermute | solution.py:276
  75.1 8.5 %collective-permute-start.3 = (bf16[4,1,1,1,24,1280]{5,4,3,2,1,0:T(8,128)(2,1)S(1)}, bf16[4,1,1,1,24,1280]{5,4,3,2,1,0:T(8,128)(2,1)S(1)}, u32[]{:S(2)}, u32[]{:S(2)}) collective-permute-start(bf16[4,1,1,1,24,1280]{5,4,3,2,1,0:T(8,128)(2,1)S(1)} %dynamic-slice_bitcast_fusion), channel_id=1, source_target_pairs={{0,8},{4,12},{8,0},{12,4},{16,24},{20,28},{24,16},{28,20},{1,9},{5... | collective-permute-start | bytes 737288 | tf_op jit(solution)/shard_map/ppermute | solution.py:276
  77.8 9.5 %collective-permute-start.16 = (bf16[4,1,2,1,24,768]{5,4,3,2,1,0:T(8,128)(2,1)S(1)}, bf16[4,1,2,1,24,768]{5,4,3,2,1,0:T(8,128)(2,1)S(1)}, u32[]{:S(2)}, u32[]{:S(2)}) collective-permute-start(bf16[4,1,2,1,24,768]{5,4,3,2,1,0:T(8,128)(2,1)S(1)} %pad_maximum_fusion.14), channel_id=1, source_target_pairs={{0,16},{4,20},{8,24},{12,28},{16,0},{20,4},{24,8},{28,12},{1,17},{... | collective-permute-start | bytes 884744 | tf_op jit(solution)/shard_map/ppermute | solution.py:276
  83.7 8.3 %collective-permute-start.10 = (bf16[4,2,1,1,24,1152]{5,4,3,2,1,0:T(8,128)(2,1)S(1)}, bf16[4,2,1,1,24,1152]{5,4,3,2,1,0:T(8,128)(2,1)S(1)}, u32[]{:S(2)}, u32[]{:S(2)}) collective-permute-start(bf16[4,2,1,1,24,1152]{5,4,3,2,1,0:T(8,128)(2,1)S(1)} %pad_maximum_fusion.12), channel_id=1, source_target_pairs={{0,8},{4,12},{8,0},{12,4},{16,24},{20,28},{24,16},{28,20},{1,9},{5... | collective-permute-start | bytes 1327112 | tf_op jit(solution)/shard_map/ppermute | solution.py:276
  87.3 8.8 %collective-permute-start.4 = (bf16[4,1,2,1,24,1280]{5,4,3,2,1,0:T(8,128)(2,1)S(1)}, bf16[4,1,2,1,24,1280]{5,4,3,2,1,0:T(8,128)(2,1)S(1)}, u32[]{:S(2)}, u32[]{:S(2)}) collective-permute-start(bf16[4,1,2,1,24,1280]{5,4,3,2,1,0:T(8,128)(2,1)S(1)} %pad_maximum_fusion.10), channel_id=1, source_target_pairs={{0,16},{4,20},{8,24},{12,28},{16,0},{20,4},{24,8},{28,12},{1,17},{... | collective-permute-start | bytes 1474568 | tf_op jit(solution)/shard_map/ppermute | solution.py:276
  144.1 45.7 %collective-permute-start.20 = (bf16[320,768]{1,0:T(8,128)(2,1)S(1)}, bf16[320,768]{1,0:T(8,128)(2,1)S(1)}, u32[]{:S(2)}, u32[]{:S(2)}) collective-permute-start(bf16[320,768]{1,0:T(8,128)(2,1)S(1)} %convolution_convert_fusion.9), channel_id=1, source_target_pairs={{0,2},{1,3},{2,0},{3,1},{4,6},{5,7},{6,4},{7,5},{8,10},{9,11},{10,... | collective-permute-start | bytes 1474568 | tf_op jit(solution)/shard_map/ppermute | solution.py:281
  153.9 25.1 %collective-permute-start.22 = (bf16[320,768]{1,0:T(8,128)(2,1)S(1)}, bf16[320,768]{1,0:T(8,128)(2,1)S(1)}, u32[]{:S(2)}, u32[]{:S(2)}) collective-permute-start(bf16[320,768]{1,0:T(8,128)(2,1)S(1)} %convolution_convert_fusion.7), channel_id=1, source_target_pairs={{0,1},{1,2},{2,3},{3,0},{4,5},{5,6},{6,7},{7,4},{8,9},{9,10},{10,1... | collective-permute-start | bytes 1474568 | tf_op jit(solution)/shard_map/ppermute | solution.py:281
  166.0 34.8 %collective-permute-start.18 = (bf16[320,768]{1,0:T(8,128)(2,1)S(1)}, bf16[320,768]{1,0:T(8,128)(2,1)S(1)}, u32[]{:S(2)}, u32[]{:S(2)}) collective-permute-start(bf16[320,768]{1,0:T(8,128)(2,1)S(1)} %convolution_convert_fusion.11), channel_id=1, source_target_pairs={{0,3},{1,0},{2,1},{3,2},{4,7},{5,4},{6,5},{7,6},{8,11},{9,8},{10,9... | collective-permute-start | bytes 1474568 | tf_op jit(solution)/shard_map/ppermute | solution.py:281
  224.3 254.1 %reduce-scatter.5.cloned.1.call-start = ((), (), s32[]{:S(2)}) async-start(), calls=%async_computation.4 | async-start | bytes 5308416 | tf_op jit(solution)/shard_map/reduce_scatter | solution.py:343
  239.4 147.8 %collective-permute-start.26 = (bf16[320,768]{1,0:T(8,128)(2,1)}, bf16[320,768]{1,0:T(8,128)(2,1)}, u32[]{:S(2)}, u32[]{:S(2)}) collective-permute-start(bf16[320,768]{1,0:T(8,128)(2,1)} %fusion.61), channel_id=1, source_target_pairs={{0,1},{1,2},{2,3},{3,0},{4,5},{5,6},{6,7},{7,4},{8,9},{9,10},{10,1... | collective-permute-start | bytes 1474568 | tf_op jit(solution)/shard_map/ppermute | solution.py:281
  263.4 123.8 %collective-permute-start.25 = (bf16[320,768]{1,0:T(8,128)(2,1)}, bf16[320,768]{1,0:T(8,128)(2,1)}, u32[]{:S(2)}, u32[]{:S(2)}) collective-permute-start(bf16[320,768]{1,0:T(8,128)(2,1)} %fusion.56), channel_id=1, source_target_pairs={{0,2},{1,3},{2,0},{3,1},{4,6},{5,7},{6,4},{7,5},{8,10},{9,11},{10,... | collective-permute-start | bytes 1474568 | tf_op jit(solution)/shard_map/ppermute | solution.py:281
  265.4 25.9 %collective-permute-start.29 = (bf16[320,768]{1,0:T(8,128)(2,1)}, bf16[320,768]{1,0:T(8,128)(2,1)}, u32[]{:S(2)}, u32[]{:S(2)}) collective-permute-start(bf16[320,768]{1,0:T(8,128)(2,1)} %get-tuple-element.155), channel_id=1, source_target_pairs={{0,1},{1,2},{2,3},{3,0},{4,5},{5,6},{6,7},{7,4},{8,9},{9,10},{10,1... | collective-permute-start | bytes 1474568 | tf_op jit(solution)/shard_map/ppermute | solution.py:281
  265.8 55.2 %collective-permute-start.28 = (bf16[320,768]{1,0:T(8,128)(2,1)}, bf16[320,768]{1,0:T(8,128)(2,1)}, u32[]{:S(2)}, u32[]{:S(2)}) collective-permute-start(bf16[320,768]{1,0:T(8,128)(2,1)} %get-tuple-element.154), channel_id=1, source_target_pairs={{0,2},{1,3},{2,0},{3,1},{4,6},{5,7},{6,4},{7,5},{8,10},{9,11},{10,... | collective-permute-start | bytes 1474568 | tf_op jit(solution)/shard_map/ppermute | solution.py:281
  268.7 52.2 %collective-permute-start.27 = (bf16[320,768]{1,0:T(8,128)(2,1)S(1)}, bf16[320,768]{1,0:T(8,128)(2,1)}, u32[]{:S(2)}, u32[]{:S(2)}) collective-permute-start(bf16[320,768]{1,0:T(8,128)(2,1)S(1)} %get-tuple-element.153), channel_id=1, source_target_pairs={{0,3},{1,0},{2,1},{3,2},{4,7},{5,4},{6,5},{7,6},{8,11},{9,8},{10,9... | collective-permute-start | bytes 1474568 | tf_op jit(solution)/shard_map/ppermute | solution.py:281
  280.1 243.8 %all-gather.3.cloned.1.call-start = ((), (), s32[]{:S(2)}) async-start(), calls=%async_computation.3 | async-start | bytes 5308416 | tf_op jit(solution)/shard_map/all_gather | solution.py:344
  291.2 95.9 %collective-permute-start.24 = (bf16[320,768]{1,0:T(8,128)(2,1)}, bf16[320,768]{1,0:T(8,128)(2,1)}, u32[]{:S(2)}, u32[]{:S(2)}) collective-permute-start(bf16[320,768]{1,0:T(8,128)(2,1)} %fusion.51), channel_id=1, source_target_pairs={{0,3},{1,0},{2,1},{3,2},{4,7},{5,4},{6,5},{7,6},{8,11},{9,8},{10,9... | collective-permute-start | bytes 1474568 | tf_op jit(solution)/shard_map/ppermute | solution.py:281
  367.3 40.9 %collective-permute-start.39 = (bf16[4,2,2,1,24,1152]{5,4,3,2,1,0:T(8,128)(2,1)}, bf16[4,2,2,1,24,1152]{5,4,3,2,1,0:T(8,128)(2,1)}, u32[]{:S(2)}, u32[]{:S(2)}) collective-permute-start(bf16[4,2,2,1,24,1152]{5,4,3,2,1,0:T(8,128)(2,1)} %constant_dynamic-slice_fusion.11), channel_id=1, source_target_pairs={{0,4},{4,0},{8,12},{12,8},{16,20},{20,16},{24,28},{28,24},{1,5},{5... | collective-permute-start | bytes 2654216 | tf_op jit(solution)/shard_map/ppermute | solution.py:276
  377.6 153.7 %all-gather.5.cloned.1.call-start = ((), (), s32[]{:S(2)}) async-start(), calls=%async_computation.5 | async-start | bytes 5308416 | tf_op jit(solution)/shard_map/all_gather | solution.py:344
  378.8 14.8 %collective-permute-start.48 = (bf16[4,2,2,1,24,768]{5,4,3,2,1,0:T(8,128)(2,1)}, bf16[4,2,2,1,24,768]{5,4,3,2,1,0:T(8,128)(2,1)}, u32[]{:S(2)}, u32[]{:S(2)}) collective-permute-start(bf16[4,2,2,1,24,768]{5,4,3,2,1,0:T(8,128)(2,1)} %constant_dynamic-slice_fusion.5), channel_id=1, source_target_pairs={{0,4},{4,0},{8,12},{12,8},{16,20},{20,16},{24,28},{28,24},{1,5},{5... | collective-permute-start | bytes 1769480 | tf_op jit(solution)/shard_map/ppermute | solution.py:276
  394.8 11.8 %collective-permute-start.49 = (bf16[4,2,1,1,24,768]{5,4,3,2,1,0:T(8,128)(2,1)S(1)}, bf16[4,2,1,1,24,768]{5,4,3,2,1,0:T(8,128)(2,1)S(1)}, u32[]{:S(2)}, u32[]{:S(2)}) collective-permute-start(bf16[4,2,1,1,24,768]{5,4,3,2,1,0:T(8,128)(2,1)S(1)} %constant_dynamic-slice_fusion.4), channel_id=1, source_target_pairs={{0,8},{4,12},{8,0},{12,4},{16,24},{20,28},{24,16},{28,20},{1,9},{5... | collective-permute-start | bytes 884744 | tf_op jit(solution)/shard_map/ppermute | solution.py:276
  406.0 44.4 %collective-permute-start.30 = (bf16[4,2,2,1,24,1280]{5,4,3,2,1,0:T(8,128)(2,1)S(1)}, bf16[4,2,2,1,24,1280]{5,4,3,2,1,0:T(8,128)(2,1)S(1)}, u32[]{:S(2)}, u32[]{:S(2)}) collective-permute-start(bf16[4,2,2,1,24,1280]{5,4,3,2,1,0:T(8,128)(2,1)S(1)} %fusion.70), channel_id=1, source_target_pairs={{0,4},{4,0},{8,12},{12,8},{16,20},{20,16},{24,28},{28,24},{1,5},{5... | collective-permute-start | bytes 2949128 | tf_op jit(solution)/shard_map/ppermute | solution.py:276
  406.7 8.0 %collective-permute-start.50 = (bf16[4,1,1,1,24,768]{5,4,3,2,1,0:T(8,128)(2,1)S(1)}, bf16[4,1,1,1,24,768]{5,4,3,2,1,0:T(8,128)(2,1)S(1)}, u32[]{:S(2)}, u32[]{:S(2)}) collective-permute-start(bf16[4,1,1,1,24,768]{5,4,3,2,1,0:T(8,128)(2,1)S(1)} %constant_dynamic-slice_fusion.3), channel_id=1, source_target_pairs={{0,16},{4,20},{8,24},{12,28},{16,0},{20,4},{24,8},{28,12},{1,17},{... | collective-permute-start | bytes 442376 | tf_op jit(solution)/shard_map/ppermute | solution.py:276
  414.8 30.5 %collective-permute-start.53 = (bf16[1,1,1,1,24,768]{5,4,3,2,1,0:T(8,128)(2,1)S(1)}, bf16[1,1,1,1,24,768]{5,4,3,2,1,0:T(8,128)(2,1)S(1)}, u32[]{:S(2)}, u32[]{:S(2)}) collective-permute-start(bf16[1,1,1,1,24,768]{5,4,3,2,1,0:T(8,128)(2,1)S(1)} %get-tuple-element.247), channel_id=1, source_target_pairs={{0,3},{1,0},{2,1},{3,2},{4,7},{5,4},{6,5},{7,6},{8,11},{9,8},{10,9... | collective-permute-start | bytes 110600 | tf_op jit(solution)/shard_map/ppermute | solution.py:281
  443.9 17.3 %collective-permute-start.40 = (bf16[4,1,2,1,24,1152]{5,4,3,2,1,0:T(8,128)(2,1)S(1)}, bf16[4,1,2,1,24,1152]{5,4,3,2,1,0:T(8,128)(2,1)S(1)}, u32[]{:S(2)}, u32[]{:S(2)}) collective-permute-start(bf16[4,1,2,1,24,1152]{5,4,3,2,1,0:T(8,128)(2,1)S(1)} %constant_dynamic-slice_fusion.10), channel_id=1, source_target_pairs={{0,16},{4,20},{8,24},{12,28},{16,0},{20,4},{24,8},{28,12},{1,17},{... | collective-permute-start | bytes 1327112 | tf_op jit(solution)/shard_map/ppermute | solution.py:276
  449.0 6.8 %collective-permute-start.54 = (bf16[1,1,1,1,24,768]{5,4,3,2,1,0:T(8,128)(2,1)S(1)}, bf16[1,1,1,1,24,768]{5,4,3,2,1,0:T(8,128)(2,1)S(1)}, u32[]{:S(2)}, u32[]{:S(2)}) collective-permute-start(bf16[1,1,1,1,24,768]{5,4,3,2,1,0:T(8,128)(2,1)S(1)} %add_convert_fusion.12), channel_id=1, source_target_pairs={{0,16},{4,20},{8,24},{12,28},{16,0},{20,4},{24,8},{28,12},{1,17},{... | collective-permute-start | bytes 110600 | tf_op jit(solution)/shard_map/ppermute | solution.py:276
  457.3 20.9 %collective-permute-start.31 = (bf16[4,2,1,1,24,1280]{5,4,3,2,1,0:T(8,128)(2,1)S(1)}, bf16[4,2,1,1,24,1280]{5,4,3,2,1,0:T(8,128)(2,1)S(1)}, u32[]{:S(2)}, u32[]{:S(2)}) collective-permute-start(bf16[4,2,1,1,24,1280]{5,4,3,2,1,0:T(8,128)(2,1)S(1)} %constant_dynamic-slice_fusion.16), channel_id=1, source_target_pairs={{0,8},{4,12},{8,0},{12,4},{16,24},{20,28},{24,16},{28,20},{1,9},{5... | collective-permute-start | bytes 1474568 | tf_op jit(solution)/shard_map/ppermute | solution.py:276
  461.4 12.4 %collective-permute-start.41 = (bf16[4,1,1,1,24,1152]{5,4,3,2,1,0:T(8,128)(2,1)S(1)}, bf16[4,1,1,1,24,1152]{5,4,3,2,1,0:T(8,128)(2,1)S(1)}, u32[]{:S(2)}, u32[]{:S(2)}) collective-permute-start(bf16[4,1,1,1,24,1152]{5,4,3,2,1,0:T(8,128)(2,1)S(1)} %constant_dynamic-slice_fusion.9), channel_id=1, source_target_pairs={{0,8},{4,12},{8,0},{12,4},{16,24},{20,28},{24,16},{28,20},{1,9},{5... | collective-permute-start | bytes 663560 | tf_op jit(solution)/shard_map/ppermute | solution.py:276
  477.7 6.0 %collective-permute-start.42 = (bf16[1,1,1,1,24,1152]{5,4,3,2,1,0:T(8,128)(2,1)S(1)}, bf16[1,1,1,1,24,1152]{5,4,3,2,1,0:T(8,128)(2,1)S(1)}, u32[]{:S(2)}, u32[]{:S(2)}) collective-permute-start(bf16[1,1,1,1,24,1152]{5,4,3,2,1,0:T(8,128)(2,1)S(1)} %get-tuple-element.241), channel_id=1, source_target_pairs={{0,1},{1,2},{2,3},{3,0},{4,5},{5,6},{6,7},{7,4},{8,9},{9,10},{10,1... | collective-permute-start | bytes 165896 | tf_op jit(solution)/shard_map/ppermute | solution.py:281
  484.7 12.3 %collective-permute-start.32 = (bf16[4,1,1,1,24,1280]{5,4,3,2,1,0:T(8,128)(2,1)S(1)}, bf16[4,1,1,1,24,1280]{5,4,3,2,1,0:T(8,128)(2,1)S(1)}, u32[]{:S(2)}, u32[]{:S(2)}) collective-permute-start(bf16[4,1,1,1,24,1280]{5,4,3,2,1,0:T(8,128)(2,1)S(1)} %constant_dynamic-slice_fusion.15), channel_id=1, source_target_pairs={{0,16},{4,20},{8,24},{12,28},{16,0},{20,4},{24,8},{28,12},{1,17},{... | collective-permute-start | bytes 737288 | tf_op jit(solution)/shard_map/ppermute | solution.py:276
  497.3 7.1 %collective-permute-start.33 = (bf16[1,1,1,1,24,1280]{5,4,3,2,1,0:T(8,128)(2,1)S(1)}, bf16[1,1,1,1,24,1280]{5,4,3,2,1,0:T(8,128)(2,1)S(1)}, u32[]{:S(2)}, u32[]{:S(2)}) collective-permute-start(bf16[1,1,1,1,24,1280]{5,4,3,2,1,0:T(8,128)(2,1)S(1)} %get-tuple-element.236), channel_id=1, source_target_pairs={{0,1},{1,2},{2,3},{3,0},{4,5},{5,6},{6,7},{7,4},{8,9},{9,10},{10,1... | collective-permute-start | bytes 184328 | tf_op jit(solution)/shard_map/ppermute | solution.py:281
  499.3 7.8 %collective-permute-start.46 = (bf16[1,1,2,1,24,1152]{5,4,3,2,1,0:T(8,128)(2,1)S(1)}, bf16[1,1,2,1,24,1152]{5,4,3,2,1,0:T(8,128)(2,1)S(1)}, u32[]{:S(2)}, u32[]{:S(2)}) collective-permute-start(bf16[1,1,2,1,24,1152]{5,4,3,2,1,0:T(8,128)(2,1)S(1)} %pad_maximum_fusion.20), channel_id=1, source_target_pairs={{0,16},{4,20},{8,24},{12,28},{16,0},{20,4},{24,8},{28,12},{1,17},{... | collective-permute-start | bytes 331784 | tf_op jit(solution)/shard_map/ppermute | solution.py:276
  504.5 6.0 %collective-permute-start.36 = (bf16[1,1,1,1,24,1280]{5,4,3,2,1,0:T(8,128)(2,1)S(1)}, bf16[1,1,1,1,24,1280]{5,4,3,2,1,0:T(8,128)(2,1)S(1)}, u32[]{:S(2)}, u32[]{:S(2)}) collective-permute-start(bf16[1,1,1,1,24,1280]{5,4,3,2,1,0:T(8,128)(2,1)S(1)} %add_convert_fusion.10), channel_id=1, source_target_pairs={{0,16},{4,20},{8,24},{12,28},{16,0},{20,4},{24,8},{28,12},{1,17},{... | collective-permute-start | bytes 184328 | tf_op jit(solution)/shard_map/ppermute | solution.py:276
  510.6 7.6 %collective-permute-start.37 = (bf16[1,2,1,1,24,1280]{5,4,3,2,1,0:T(8,128)(2,1)S(1)}, bf16[1,2,1,1,24,1280]{5,4,3,2,1,0:T(8,128)(2,1)S(1)}, u32[]{:S(2)}, u32[]{:S(2)}) collective-permute-start(bf16[1,2,1,1,24,1280]{5,4,3,2,1,0:T(8,128)(2,1)S(1)} %pad_maximum_fusion.19), channel_id=1, source_target_pairs={{0,8},{4,12},{8,0},{12,4},{16,24},{20,28},{24,16},{28,20},{1,9},{5... | collective-permute-start | bytes 368648 | tf_op jit(solution)/shard_map/ppermute | solution.py:276
  510.7 7.6 %collective-permute-start.47 = (bf16[1,2,2,1,24,1152]{5,4,3,2,1,0:T(8,128)(2,1)S(1)}, bf16[1,2,2,1,24,1152]{5,4,3,2,1,0:T(8,128)(2,1)S(1)}, u32[]{:S(2)}, u32[]{:S(2)}) collective-permute-start(bf16[1,2,2,1,24,1152]{5,4,3,2,1,0:T(8,128)(2,1)S(1)} %pad_maximum_fusion.17), channel_id=1, source_target_pairs={{0,4},{4,0},{8,12},{12,8},{16,20},{20,16},{24,28},{28,24},{1,5},{5... | collective-permute-start | bytes 663560 | tf_op jit(solution)/shard_map/ppermute | solution.py:276
  (76 other events, 890.6 us)
Sparse Core Ops, SparseCore 0:
  224.4 70.1 reduce-scatter.2
  299.1 53.8 reduce-scatter.4
  377.7 66.1 all-gather.2
  478.6 42.2 all-gather.4
